TPU v7x, 128 devices: a whole 4x4x4 slice. The times are simulated.
128 devices in a mesh: member: 8 (over x, core), space: 16 (over z, y).
Axes of the slice: x: 4, y: 4, z: 4, core: 2. Of those that a mesh axis runs over, the one named last changes fastest.
Arguments:
- spectra: float32 [32, 12, 320, 641], P('member', None, 'space'), may hold values from -6 to 6
- legendre: bfloat16 [320, 641, 384], P('space'), as said below
- sin_lat: float32 [384], replicated, may hold values from 0 to 1, as said below
- gravity: float32 [2, 2], replicated, may hold values from 0.1 to 2, as said below
- stability: float32 [2, 2], replicated, may hold values from 0.1 to 2, as said below
- clones: int32 [4, 2], replicated, may hold values from 0 to 31, as said below
Outputs:
- new_state: float32 [32, 12, 320, 641], P('member', None, 'space')
Inputs may be any that keep to these rules, and one draw needn't show every extreme that they name: `clones`: column 0 holds 4 distinct killed trajectories, column 1 for each a survivor; no survivor is killed, and a survivor may be copied onto several killed trajectories. legendre[p, j, l] is the associated Legendre function of the (m, n) of position (p, j), normalized so that its square integrates to one over -1 to 1, at mu = sin_lat[l]. `sin_lat`: decreasing from the pole towards the equator. `gravity`: diagonal entries 1 to 2, off-diagonal entries 0.1 to 0.6. `stability`: diagonal entries 1 to 2, off-diagonal entries 0.1 to 0.6.
All inputs are finite; a program needn't handle non-finite values.
Results may differ from a plain program's by a relative error of at most 0.0016.
Values may be sent and summed in bfloat16 or wider, within the bound.
A program may use at most 128 MiB of HBM per device.

v0:
```python
import math

import jax
import jax.numpy as jnp
from jax import lax
from jax.sharding import PartitionSpec as P

NLON = 1280


time_step = 0.25
wave_scale = 16.0
diffusion = 0.02


def from_root(value, axis, root):
    mine = lax.axis_index(axis) == root
    return lax.psum(jnp.where(mine, value, jnp.zeros_like(value)), axis)


def pair_layout(pair_index, row_length, truncation):
    column = jnp.arange(row_length, dtype=jnp.int32)[None, :]
    lower_pair = pair_index[:, None]
    leading = column < truncation - lower_pair
    wave_order = jnp.where(leading, lower_pair, truncation - 1 - lower_pair)
    offset = jnp.where(leading, column, column - (truncation - lower_pair))
    parity = (1 - 2 * (offset % 2)).astype(jnp.float32)
    return (leading.astype(jnp.float32), parity, wave_order + offset)


def fourier_table(pair_count, truncation, longitudes):
    halves = jnp.arange(2, dtype=jnp.int32)[:, None]
    pair_all = jnp.arange(pair_count, dtype=jnp.int32)[None, :]
    wave_order = jnp.where(halves == 0, pair_all, truncation - 1 - pair_all)
    column = jnp.arange(longitudes, dtype=jnp.int32)
    phase = wave_order[:, :, None] * column[None, None, :] % longitudes
    angle = phase.astype(jnp.float32) * (2.0 * math.pi / longitudes)
    return jnp.stack([jnp.cos(angle), -jnp.sin(angle)]).astype(jnp.bfloat16)


def latitude_terms(sin_lat, first_row, count):
    mirrored = jnp.concatenate([sin_lat, -sin_lat])
    local_sine = lax.dynamic_slice_in_dim(mirrored, first_row, count)
    weights = math.pi * jnp.sqrt(1.0 - local_sine * local_sine) / mirrored.shape[0]
    return (2.0 * local_sine, weights)


def tendencies(physical_grid_samples, coriolis):
    local_spin_spectrum = physical_grid_samples[:, 0:2]
    spreading_rate_spectrum = physical_grid_samples[:, 2:4]
    thermal_spectrum = physical_grid_samples[:, 4:6]
    planetary_spin_spectrum = local_spin_spectrum + coriolis[:, None]
    average_heat_level = 0.5 * (thermal_spectrum[:, 0:1] + thermal_spectrum[:, 1:2])
    return jnp.concatenate(
        [
            -planetary_spin_spectrum * spreading_rate_spectrum,
            planetary_spin_spectrum * local_spin_spectrum
            - 0.5 * spreading_rate_spectrum * spreading_rate_spectrum,
            -(thermal_spectrum + average_heat_level) * spreading_rate_spectrum,
        ],
        axis=1,
    )


def semi_implicit(spectra, tendency, degree, gravity, stability):
    trajectory_count, comp_count, pair_count, row_length = spectra.shape
    truncation = row_length - 1
    shaped = spectra.reshape(trajectory_count, comp_count // 2, 2, pair_count, row_length)
    forcing = tendency.reshape(trajectory_count, comp_count // 2, 2, pair_count, row_length)
    eigen_value = (
        wave_scale * (degree * (degree + 1)).astype(jnp.float32) / float(truncation * truncation)
    )
    damping = 1.0 / (1.0 + diffusion * eigen_value * eigen_value)
    coupling = time_step * time_step * eigen_value
    product = jnp.dot(gravity, stability, precision=lax.Precision.HIGHEST)
    new_zeta = damping * (shaped[:, 0:2] + time_step * forcing[:, 0:2])
    t_star = shaped[:, 4:6] + time_step * forcing[:, 4:6]
    d_star = shaped[:, 2:4] + time_step * forcing[:, 2:4]
    right_one = d_star[:, 0] + time_step * eigen_value * (
        gravity[0, 0] * t_star[:, 0] + gravity[0, 1] * t_star[:, 1]
    )
    right_two = d_star[:, 1] + time_step * eigen_value * (
        gravity[1, 0] * t_star[:, 0] + gravity[1, 1] * t_star[:, 1]
    )
    diag_one = 1.0 + coupling * product[0, 0]
    diag_two = 1.0 + coupling * product[1, 1]
    cross_one = coupling * product[0, 1]
    cross_two = coupling * product[1, 0]
    determ = diag_one * diag_two - cross_one * cross_two
    div_one = (diag_two * right_one - cross_one * right_two) / determ
    div_two = (diag_one * right_two - cross_two * right_one) / determ
    temp_one = damping * (
        t_star[:, 0] - time_step * (stability[0, 0] * div_one + stability[0, 1] * div_two)
    )
    temp_two = damping * (
        t_star[:, 1] - time_step * (stability[1, 0] * div_one + stability[1, 1] * div_two)
    )
    new_div = damping * jnp.stack([div_one, div_two], axis=1)
    new_temp = jnp.stack([temp_one, temp_two], axis=1)
    result = jnp.concatenate([new_zeta, new_div, new_temp], axis=1)
    return result.reshape(spectra.shape)


def advance(spectra, legendre, sin_lat, gravity, stability):
    trajectory_count, comp_count, pair_local, row_length = spectra.shape
    space_count = lax.axis_size("space")
    position = lax.axis_index("space")
    truncation = row_length - 1
    half_lat = legendre.shape[2]
    lat_count = 2 * half_lat
    lat_local = lat_count // space_count
    pair_total = pair_local * space_count
    pair_index = position * pair_local + jnp.arange(pair_local, dtype=jnp.int32)
    leading, parity, degree = pair_layout(pair_index, row_length, truncation)
    halves = jnp.stack([leading, 1.0 - leading])
    mirror_sign = jnp.stack([jnp.ones_like(parity), parity])
    factor = (halves[:, None] * mirror_sign[None, :]).astype(jnp.bfloat16)
    inputs = spectra.astype(jnp.bfloat16)[:, :, None, None] * factor[None, None]
    fourier = jnp.einsum("tchspj,pjl->tchpsl", inputs, legendre, preferred_element_type=jnp.float32)
    fourier = fourier.reshape(trajectory_count, comp_count, 2, pair_local, lat_count).astype(
        jnp.bfloat16
    )
    zonal_table = fourier_table(pair_total, truncation, NLON)
    coriolis, weights = latitude_terms(sin_lat, position * lat_local, lat_local)
    banded = lax.all_to_all(fourier, "space", split_axis=4, concat_axis=3, tiled=True)
    grid_banded = banded
    count_here = grid_banded.shape[0]
    grid_banded = grid_banded.reshape(count_here, comp_count // 2, 2, 2, pair_total, lat_local)
    physical_grid_samples = jnp.einsum(
        "tfrhpl,rhpk->tflk", grid_banded, zonal_table, preferred_element_type=jnp.float32
    ) * (1.0 / truncation)
    forcing = tendencies(physical_grid_samples, coriolis).astype(jnp.bfloat16)
    weighted = (
        jnp.einsum("tflk,rhpk->tfrhpl", forcing, zonal_table, preferred_element_type=jnp.float32)
        * weights
    )
    returned = lax.all_to_all(
        weighted.astype(jnp.bfloat16).reshape(count_here, comp_count, 2, pair_total, lat_local),
        "space",
        split_axis=3,
        concat_axis=4,
        tiled=True,
    )
    returned = returned.reshape(trajectory_count, comp_count, 2, pair_local, 2, half_lat).astype(
        jnp.float32
    )
    legendre_wide = legendre.astype(jnp.float32)
    projected = jnp.einsum(
        "tchpsl,pjl->tchspj", returned, legendre_wide, precision=lax.Precision.HIGHEST
    )
    first_part = projected[:, :, 0, 0] + parity * projected[:, :, 0, 1]
    second_part = projected[:, :, 1, 0] + parity * projected[:, :, 1, 1]
    tendency = leading * first_part + (1.0 - leading) * second_part
    return semi_implicit(spectra, tendency, degree, gravity, stability)


def copy_clones(field_values, clones):
    resident_rows = field_values.shape[0]
    ensemble_slot = lax.axis_index("member")
    row_numbers = jnp.arange(resident_rows, dtype=jnp.int32)

    def visit(entry, updated):
        removed_members = clones[entry, 0]
        sending_member = clones[entry, 1]
        owning_member = sending_member // resident_rows
        surviving_member = lax.dynamic_index_in_dim(
            field_values, sending_member % resident_rows, 0, keepdims=False
        )
        received_rows = from_root(surviving_member, "member", owning_member)
        is_mine = removed_members // resident_rows == ensemble_slot
        selected = jnp.logical_and(row_numbers == removed_members % resident_rows, is_mine)
        return jnp.where(selected[:, None, None, None], received_rows[None], updated)

    return lax.fori_loop(0, clones.shape[0], visit, field_values)


def shards(spectra, legendre, sin_lat, gravity, stability, clones):
    advanced_states = advance(spectra, legendre, sin_lat, gravity, stability)
    return copy_clones(advanced_states, clones)


def solution(mesh):
    placed = (P("member", None, "space", None), P("space", None, None), P(), P(), P(), P())
    return jax.shard_map(
        shards,
        mesh=mesh,
        in_specs=placed,
        out_specs=P("member", None, "space", None),
        check_vma=False,
    )
```

profile of v0, /device:TPU:1, one launch (start us, length us, event | category | flops | bytes accessed | tf_op | source)
XLA Modules:
  0.0 712.8 jit_solution(2429236175083270238)
XLA Ops:
  6.8 0.3 fusion.60
  7.1 2.3 convert_element_type.116
  9.5 0.5 copy.49
  10.3 9.5 %convert_bitcast_fusion = bf16[4,12,2,20,2,384]{5,1,4,2,0,3:T(8,128)(2,1)} fusion(bf16[20,641,384]{2,1,0:T(8,128)(2,1)} %param.9, bf16[2,2,20,641]{3,1,0,2:T(2,128)(2,1)S(1)} %multiply_convert_fusion.1, bf16[4,12,20,641]{3,1,0,2:T(8,128)(2,1)S(1)} %copy.49), kind=kOutput, calls=%fused_computation.20 | convolution fusion | flops 1894321920 | bytes 14128160 | tf_op jit(solution)/shard_map/tchspj,pjl->tchpsl/dot_general | solution.py:119
  19.8 36.2 %copy.75 = bf16[4,12,2,20,2,384]{3,0,2,1,5,4:T(4,128)(2,1)} copy(bf16[4,12,2,20,2,384]{5,1,4,2,0,3:T(8,128)(2,1)} %convert_bitcast_fusion) | data formatting | bytes 5898240 | tf_op jit(solution)/shard_map/convert_element_type | solution.py:120
  56.0 39.0 %reshape.950 = bf16[16,2,46080]{2,1,0:T(2,128)(2,1)} reshape(bf16[768,12,2,4,20]{4,3,2,1,0:T(4,128)(2,1)} %bitcast.82) | data formatting | bytes 5898240
  95.0 8.9 %all-to-all-start = ((bf16[16,2,46080]{2,1,0:T(2,128)(2,1)}), bf16[16,2,46080]{2,1,0:T(2,128)(2,1)S(1)}, u32[]{:S(2)}, u32[]{:S(2)}) async-start(bf16[16,2,46080]{2,1,0:T(2,128)(2,1)} %reshape.950), calls=%async_computation | async-start | bytes 5898240 | tf_op jit(solution)/shard_map/all_to_all | solution.py:125
  104.2 15.8 %cosine_convert_fusion = (bf16[1,2,320,1280]{3,2,0,1:T(8,128)(2,1)}, bf16[1,2,320,1280]{3,2,0,1:T(8,128)(2,1)}) fusion(s32[2,320]{1,0:T(2,128)S(1)} %iota_select_fusion), kind=kLoop, calls=%fused_computation.30 | loop fusion | flops 9830400 | bytes 3279360 | tf_op jit(solution)/shard_map/convert.3
  120.0 27.7 %all-to-all-done = bf16[16,2,46080]{2,1,0:T(2,128)(2,1)S(1)} async-done(((bf16[16,2,46080]{2,1,0:T(2,128)(2,1)}), bf16[16,2,46080]{2,1,0:T(2,128)(2,1)S(1)}, u32[]{:S(2)}, u32[]{:S(2)}) %all-to-all-start) | async-done | bytes 2949152 | tf_op jit(solution)/shard_map/all_to_all | solution.py:125
  147.7 47.8 %reshape.951 = bf16[768,12,2,4,20]{4,3,2,1,0:T(4,128)(2,1)} reshape(bf16[16,2,46080]{2,1,0:T(2,128)(2,1)S(1)} %all-to-all-done) | data formatting | bytes 5898240
  195.5 36.3 %copy.76 = bf16[4,12,2,20,16,48]{5,4,2,3,1,0:T(8,128)(2,1)} copy(bf16[4,12,2,20,16,48]{3,0,2,1,5,4:T(4,128)(2,1)} %bitcast.83) | data formatting | bytes 5898240 | tf_op jit(solution)/shard_map/all_to_all | solution.py:125
  231.8 11.9 %copy.53 = bf16[4,12,2,16,20,48]{5,2,4,3,1,0:T(2,128)(2,1)S(1)} copy(bf16[4,12,2,16,20,48]{5,3,2,4,1,0:T(8,128)(2,1)} %bitcast.84) | data formatting | bytes 5898240 | tf_op jit(solution)/shard_map/all_to_all | solution.py:125
  243.7 4.7 bitcast_multiply_fusion
  248.5 0.9 fusion.37
  249.5 5.1 fusion.18
  254.6 0.6 copy.56
  255.2 12.2 %copy.57 = bf16[4,12,2,320,48]{4,2,1,0,3:T(2,128)(2,1)} copy(bf16[4,12,2,320,48]{3,4,2,1,0:T(8,128)(2,1)S(1)} %bitcast.89) | data formatting | bytes 5898240 | tf_op jit(solution)/shard_map/reshape | solution.py:138
  267.4 16.2 %reshape.952 = bf16[16,2,46080]{2,1,0:T(2,128)(2,1)} reshape(bf16[320,4,12,2,48]{4,3,2,1,0:T(2,128)(2,1)} %bitcast.85) | data formatting | bytes 5898240
  283.6 3.9 all-to-all-start.1
  287.7 0.7 fusion.66
  290.7 0.7 fusion.65
  291.4 0.6 fusion.64
  292.2 0.8 multiply_add_fusion.1
  292.9 34.5 %all-to-all-done.1 = bf16[16,2,46080]{2,1,0:T(2,128)(2,1)S(1)} async-done(((bf16[16,2,46080]{2,1,0:T(2,128)(2,1)}), bf16[16,2,46080]{2,1,0:T(2,128)(2,1)S(1)}, u32[]{:S(2)}, u32[]{:S(2)}) %all-to-all-start.1) | async-done | bytes 2949152 | tf_op jit(solution)/shard_map/all_to_all | solution.py:137
  327.4 10.7 %reshape.953 = bf16[320,4,12,2,48]{4,3,2,1,0:T(2,128)(2,1)} reshape(bf16[16,2,46080]{2,1,0:T(2,128)(2,1)S(1)} %all-to-all-done.1) | data formatting | bytes 5898240
  338.1 15.4 %copy.59 = bf16[4,12,2,20,16,48]{5,4,3,2,1,0:T(8,128)(2,1)} copy(bf16[4,12,2,20,16,48]{5,2,1,0,3,4:T(2,128)(2,1)} %bitcast.86) | data formatting | bytes 5898240 | tf_op jit(solution)/shard_map/all_to_all | solution.py:137
  353.5 14.9 %reshape.943 = bf16[4,12,2,20,2,384]{5,4,3,2,1,0:T(2,128)(2,1)S(1)} reshape(bf16[4,12,2,20,16,48]{5,4,3,2,1,0:T(8,128)(2,1)} %copy.59) | data formatting | bytes 5898240 | tf_op jit(solution)/shard_map/reshape | solution.py:144
  368.5 13.3 %fusion.7 = f32[4,12,2,2,20,641]{5,1,3,2,0,4:T(8,128)} fusion(bf16[20,641,384]{2,1,0:T(8,128)(2,1)} %param.9, bf16[4,12,2,20,2,384]{5,4,3,2,1,0:T(2,128)(2,1)S(1)} %reshape.943), kind=kOutput, calls=%fused_computation.12 | convolution fusion | flops 1890385920 | bytes 22640640 | tf_op jit(solution)/shard_map/tchpsl,pjl->tchspj/dot_general | solution.py:148
  381.8 12.4 %fusion.63 = (f32[4,12,1,1,20,641]{5,1,3,2,0,4:T(8,128)}, f32[4,12,1,1,20,641]{5,1,3,2,0,4:T(8,128)}, f32[4,12,1,1,20,641]{5,1,3,2,0,4:T(8,128)}, f32[4,12,1,1,20,641]{5,1,3,2,0,4:T(8,128)}) fusion(f32[4,12,2,2,20,641]{5,1,3,2,0,4:T(8,128)} %fusion.7), kind=kLoop, calls=%fused_computation.112 | loop fusion | bytes 19691520 | tf_op jit(solution)/shard_map/slice | solution.py:151
  394.2 4.2 copy.61
  398.4 1.9 copy.62
  400.5 1.9 copy.63
  402.6 1.9 copy.64
  404.5 2.0 multiply_add_fusion
  406.6 1.1 fusion.46
  407.7 2.8 slice_add_fusion.3
  410.6 1.7 subtract_multiply_fusion.1
  412.3 0.3 maximum_multiply_fusion
  412.6 1.6 subtract_multiply_fusion
  414.1 0.8 pad_maximum_fusion
  414.9 0.6 copy.65
  415.5 1.0 copy-done
  416.5 286.0 %while.17 = (s32[]{:T(128)}, f32[4,12,20,641]{3,2,1,0:T(8,128)S(1)}, s32[4,2]{0,1:T(2,128)S(1)}, s32[]{:T(128)}, f32[4,12,20,641]{3,0,2,1:T(4,128)}, /*index=5*/...) while((s32[]{:T(128)}, ...), condition=%wide.region_2.3_spmd.clone, body=%wide.region_0.2_spmd.clone.sunk | while | flops 923096 | bytes 12231253 | solution.py:174
  416.5 0.7 constant_dynamic-slice_fusion.5
  420.0 3.5 constant_dynamic-slice_fusion.6
  423.5 2.1 fusion.71
  428.4 57.0 %all-reduce.3.cloned.1.call-done = f32[12,20,641]{2,1,0:T(8,128)} async-done(((f32[12,20,641]{2,1,0:T(8,128)}), f32[12,20,641]{2,1,0:T(8,128)}) %all-reduce.3.cloned.1.call-update) | async-done | bytes 615376 | tf_op jit(solution)/shard_map/while/body/eval_jaxpr/psum | solution.py:18
  485.3 1.7 broadcast_select_fusion.2
  487.1 0.7 constant_dynamic-slice_fusion.5
  490.6 3.5 constant_dynamic-slice_fusion.6
  494.1 2.1 fusion.71
  499.0 58.2 %all-reduce.3.cloned.1.call-done = f32[12,20,641]{2,1,0:T(8,128)} async-done(((f32[12,20,641]{2,1,0:T(8,128)}), f32[12,20,641]{2,1,0:T(8,128)}) %all-reduce.3.cloned.1.call-update) | async-done | bytes 615376 | tf_op jit(solution)/shard_map/while/body/eval_jaxpr/psum | solution.py:18
  557.1 1.7 broadcast_select_fusion.2
  558.9 0.7 constant_dynamic-slice_fusion.5
  562.4 3.5 constant_dynamic-slice_fusion.6
  565.9 2.1 fusion.71
  570.8 58.2 %all-reduce.3.cloned.1.call-done = f32[12,20,641]{2,1,0:T(8,128)} async-done(((f32[12,20,641]{2,1,0:T(8,128)}), f32[12,20,641]{2,1,0:T(8,128)}) %all-reduce.3.cloned.1.call-update) | async-done | bytes 615376 | tf_op jit(solution)/shard_map/while/body/eval_jaxpr/psum | solution.py:18
  628.9 1.7 broadcast_select_fusion.2
  630.7 0.7 constant_dynamic-slice_fusion.5
  634.2 3.5 constant_dynamic-slice_fusion.6
  637.7 2.1 fusion.71
  642.6 58.2 %all-reduce.3.cloned.1.call-done = f32[12,20,641]{2,1,0:T(8,128)} async-done(((f32[12,20,641]{2,1,0:T(8,128)}), f32[12,20,641]{2,1,0:T(8,128)}) %all-reduce.3.cloned.1.call-update) | async-done | bytes 615376 | tf_op jit(solution)/shard_map/while/body/eval_jaxpr/psum | solution.py:18
  700.8 1.7 broadcast_select_fusion.2
  702.5 3.5 copy.67
  (54 shorter events, 1.8 us)
Async XLA Ops:
  95.0 8.9 %copy-start.10 = (f32[384]{0:T(512)S(1)}, f32[384]{0:T(512)}, u32[]{:S(2)}) copy-start(f32[384]{0:T(512)} %param.10) | copy-start | bytes 4612
  95.0 52.7 %all-to-all-start = ((bf16[16,2,46080]{2,1,0:T(2,128)(2,1)}), bf16[16,2,46080]{2,1,0:T(2,128)(2,1)S(1)}, u32[]{:S(2)}, u32[]{:S(2)}) async-start(bf16[16,2,46080]{2,1,0:T(2,128)(2,1)} %reshape.950), calls=%async_computation | async-start | bytes 5898240 | tf_op jit(solution)/shard_map/all_to_all | solution.py:125
  231.8 11.9 %copy-start.5 = (bf16[1,2,320,1280]{3,2,0,1:T(8,128)(2,1)S(1)}, bf16[1,2,320,1280]{3,2,0,1:T(8,128)(2,1)}, u32[]{:S(2)}) copy-start(bf16[1,2,320,1280]{3,2,0,1:T(8,128)(2,1)} %get-tuple-element.243) | copy-start | bytes 4915204
  231.8 11.9 %copy-start.6 = (bf16[1,2,320,1280]{3,2,0,1:T(8,128)(2,1)S(1)}, bf16[1,2,320,1280]{3,2,0,1:T(8,128)(2,1)}, u32[]{:S(2)}) copy-start(bf16[1,2,320,1280]{3,2,0,1:T(8,128)(2,1)} %get-tuple-element.244) | copy-start | bytes 4915204
  283.6 3.9 copy-start.11
  283.6 3.9 copy-start.12
  283.6 43.8 %all-to-all-start.1 = ((bf16[16,2,46080]{2,1,0:T(2,128)(2,1)}), bf16[16,2,46080]{2,1,0:T(2,128)(2,1)S(1)}, u32[]{:S(2)}, u32[]{:S(2)}) async-start(bf16[16,2,46080]{2,1,0:T(2,128)(2,1)} %reshape.952), calls=%async_computation.1 | async-start | bytes 5898240 | tf_op jit(solution)/shard_map/all_to_all | solution.py:137
  394.2 4.2 copy-start.3
  398.3 2.1 copy-start.2
  400.5 2.1 copy-start.1
  404.5 2.1 copy-start.4
  406.5 1.2 copy-start.8
  406.5 4.0 copy-start.7
  414.9 1.6 copy-start
  414.9 1.6 copy-start.9
  416.5 68.8 %all-reduce.3.cloned.1.call-start = ((), (), s32[]{:S(2)}) async-start(), calls=%async_computation.2 | async-start | bytes 1769472 | tf_op jit(solution)/shard_map/while/body/eval_jaxpr/psum | solution.py:18
  487.1 70.1 %all-reduce.3.cloned.1.call-start = ((), (), s32[]{:S(2)}) async-start(), calls=%async_computation.2 | async-start | bytes 1769472 | tf_op jit(solution)/shard_map/while/body/eval_jaxpr/psum | solution.py:18
  558.9 70.1 %all-reduce.3.cloned.1.call-start = ((), (), s32[]{:S(2)}) async-start(), calls=%async_computation.2 | async-start | bytes 1769472 | tf_op jit(solution)/shard_map/while/body/eval_jaxpr/psum | solution.py:18
  630.7 70.1 %all-reduce.3.cloned.1.call-start = ((), (), s32[]{:S(2)}) async-start(), calls=%async_computation.2 | async-start | bytes 1769472 | tf_op jit(solution)/shard_map/while/body/eval_jaxpr/psum | solution.py:18
Sparse Core Ops, SparseCore 0:
  425.7 59.5 all-reduce.2
  496.3 60.7 all-reduce.2
  568.2 60.7 all-reduce.2
  640.0 60.7 all-reduce.2
where the time goes:
time: 723 us; the launch traced here: 713 us
  waiting for transfers between devices  294 us (41%)
  local copies, waits for them, and re-layouts  288 us (40%)
  other arithmetic  46.9 us (6%)
  matrix products  32.8 us (5%)
  loops' own time  22.2 us (3%)
  between operations  16 us (2%)
  starting transfers between devices  12.9 us (2%)
    psum x4, waiting for transfers between devices, from_root(): return lax.psum(jnp.where(mine, value, jnp.zeros_like(value)), axis)  231 us
    unnamed x31, local copies, waits for them, and re-layouts  116 us
    all_to_all x2, local copies, waits for them, and re-layouts, advance(): lax.all_to_all(fourier, 'space', split_axis=4, concat_axis=3, tiled=True)  48.2 us
    convert_element_type x1, local copies, waits for them, and re-layouts, advance(): fourier.reshape(trajectory_count, comp_count, 2, pair_local, lat_count)  36.2 us
    all_to_all x1, waiting for transfers between devices, advance(): lax.all_to_all(weighted.astype(jnp.bfloat16).reshape(count_here, comp_cou...  34.5 us
    all_to_all x1, waiting for transfers between devices, advance(): lax.all_to_all(fourier, 'space', split_axis=4, concat_axis=3, tiled=True)  27.7 us
    another operation x1, loops' own time, copy_clones(): return lax.fori_loop(0, clones.shape[0], visit, field_values)  22.2 us
    slice x3, local copies, waits for them, and re-layouts, advance(): first_part = projected[:, :, 0, 0] + parity * projected[:, :, 0, 1]  18.4 us
  transfers between devices with their start and end apart: 6, of which 6 were waited for; matrix products, arithmetic and copies ran while one was open for 3% of the time, Pallas kernels for 0%

commit v1 on v0

v1 whole, which is shorter than its diff:
```python
import functools
import math

import jax
import jax.numpy as jnp
import numpy as np
from jax import lax
from jax.experimental import pallas as pl
from jax.experimental.pallas import tpu as pltpu
from jax.sharding import PartitionSpec as P

NW = 640
WIDTH = NW + 1
NLON = 1280
NLAT = 768
NHALF = 384
PAIRS = 320
TRAJ = 4
FIELDS = 6
LOCAL = 20
SPACE = 16
GROUP = 4
GROUPS = LOCAL // GROUP
ROWS = 4 * LOCAL
FULL = 128 * FIELDS
LANES = FULL + 64 * FIELDS
DT = 0.25
WAVE_SCALE = 16.0
DIFFUSION = 0.02
F32 = jnp.float32
BF16 = jnp.bfloat16


@functools.cache
def zonal_tables():
    pair = np.arange(PAIRS)
    order = np.stack([pair, NW - 1 - pair], axis=1)
    phase = (order[:, :, None] * np.arange(NLON)) % NLON
    angle = phase * (2.0 * math.pi / NLON)
    table = np.stack([np.cos(angle), -np.sin(angle)], axis=2).reshape(4 * PAIRS, NLON)
    table = table.astype(jnp.bfloat16)
    return table, np.ascontiguousarray(table.T)


def row_col(rows, width):
    return (
        lax.broadcasted_iota(jnp.int32, (rows, width), 0),
        lax.broadcasted_iota(jnp.int32, (rows, width), 1),
    )


def sign_mask(pair):
    row, col = row_col(8, WIDTH)
    leading = (col < NW - pair).astype(jnp.int32)
    offset = jnp.where(leading == 1, col, col - (NW - pair))
    parity = (1 - 2 * (offset & 1)).astype(F32)
    sign = jnp.where(row >= 4, parity, 1.0)
    return jnp.where(((row >> 1) & 1) + leading == 1, sign, 0.0)


def swap4(value):
    return pltpu.roll(value, 4, 1)


def legendre_group(group, first_pair, x_ref, leg_ref, put):
    row8, _ = row_col(8, WIDTH)
    odd = (row8 & 1) == 1
    results = []
    for k in range(GROUP):
        local = group * GROUP + k
        mask = sign_mask(first_pair + local)
        pieces = []
        for t in range(TRAJ):
            for f in range(FIELDS):
                real = x_ref[t, 2 * f, pl.ds(local, 1), :]
                imag = x_ref[t, 2 * f + 1, pl.ds(local, 1), :]
                pieces.append(jnp.where(odd, imag, real) * mask)
        lhs = jnp.concatenate(pieces, axis=0).astype(BF16)
        dots = jnp.dot(lhs, leg_ref[k], preferred_element_type=F32)
        results.append(dots.reshape(TRAJ * FIELDS, 8, NHALF))
    upper = lax.broadcasted_iota(jnp.int32, (TRAJ * FIELDS, 8, NHALF), 1) < 4
    hemispheres = ([], [])
    for k in range(0, GROUP, 2):
        first, second = results[k], results[k + 1]
        hemispheres[0].append(jnp.where(upper, first, swap4(second)))
        hemispheres[1].append(jnp.where(upper, swap4(first), second))
    low = lax.broadcasted_iota(jnp.int32, (16, 128), 1) < 64
    for side in range(2):
        one, two = hemispheres[side]
        for t in range(TRAJ):
            for level in range(FIELDS // 2):
                tiles = []
                for f in (2 * level, 2 * level + 1):
                    tile = jnp.concatenate([one[t * FIELDS + f], two[t * FIELDS + f]], axis=0)
                    put(4 * t + 2 * side, 128 * f, tile[:, 0:128].astype(BF16))
                    put(4 * t + 2 * side + 1, 128 * f, tile[:, 128:256].astype(BF16))
                    tiles.append(tile[:, 256:384])
                a, b = tiles
                lane = FULL + 128 * level
                put(4 * t + 2 * side, lane, jnp.where(low, a, pltpu.roll(b, 64, 1)).astype(BF16))
                put(
                    4 * t + 2 * side + 1, lane, jnp.where(low, pltpu.roll(a, 64, 1), b).astype(BF16)
                )


def legendre_kernel(x_ref, leg_ref, out_ref):
    group = pl.program_id(0)
    first_pair = lax.axis_index("space") * LOCAL

    def put(block, lane, value):
        out_ref[block, :, lane : lane + 128] = value

    legendre_group(group, first_pair, x_ref, leg_ref, put)


def latitude_rows(sin_ref, place):
    low = lax.broadcasted_iota(jnp.int32, (1, 128), 1) < 64
    zero, one, two = (sin_ref[:, 128 * i : 128 * i + 128] for i in range(3))
    swapped = pltpu.roll(two, 64, 1)
    second = (place & 1) == 1
    sign = jnp.where((place & 3) >= 2, -1.0, 1.0).astype(F32)
    full = jnp.where(second, one, zero) * sign
    half = jnp.where(second, jnp.where(low, swapped, two), jnp.where(low, two, swapped)) * sign
    return full, half


def forcing_of(spin, spread, heat, heat_swapped, coriolis):
    spun = spin + coriolis
    return (
        -spun * spread,
        spun * spin - 0.5 * spread * spread,
        -(heat + 0.5 * (heat + heat_swapped)) * spread,
    )


def grid_kernel(f_ref, tall_ref, wide_ref, sin_ref, out_ref, forcing_ref):
    place = lax.axis_index("space")
    full, half = latitude_rows(sin_ref, place)
    tile = 256

    def forward(i, _):
        rows = pl.ds(pl.multiple_of(i * tile, tile), tile)
        basis = wide_ref[rows, :]
        part = jnp.dot(basis, f_ref[:, 0:FULL], preferred_element_type=F32) * (1.0 / NW)
        field = [part[:, 128 * f : 128 * f + 128] for f in range(FIELDS)]
        for a in range(2):
            made = forcing_of(field[a], field[2 + a], field[4 + a], field[5 - a], 2.0 * full)
            for g in range(3):
                lane = 128 * (2 * g + a)
                forcing_ref[rows, lane : lane + 128] = made[g].astype(BF16)
        part = jnp.dot(basis, f_ref[:, FULL:LANES], preferred_element_type=F32) * (1.0 / NW)
        field = [part[:, 128 * f : 128 * f + 128] for f in range(3)]
        made = forcing_of(*field, pltpu.roll(field[2], 64, 1), 2.0 * half)
        for g in range(3):
            lane = FULL + 128 * g
            forcing_ref[rows, lane : lane + 128] = made[g].astype(BF16)
        return 0

    lax.fori_loop(0, NLON // tile, forward, 0)
    weight_full = math.pi * jnp.sqrt(1.0 - full * full) / NLAT
    weight_half = math.pi * jnp.sqrt(1.0 - half * half) / NLAT
    weights = jnp.concatenate([weight_full] * FIELDS + [weight_half] * 3, axis=1)

    def backward(i, _):
        rows = pl.ds(pl.multiple_of(i * tile, tile), tile)
        basis = tall_ref[rows, :]
        part = jnp.dot(basis, forcing_ref[:, 0:FULL], preferred_element_type=F32)
        out_ref[rows, 0:FULL] = (part * weights[:, 0:FULL]).astype(BF16)
        part = jnp.dot(basis, forcing_ref[:, FULL:LANES], preferred_element_type=F32)
        out_ref[rows, FULL:LANES] = (part * weights[:, FULL:LANES]).astype(BF16)
        return 0

    lax.fori_loop(0, 4 * PAIRS // tile, backward, 0)


def project_group(group, first_pair, get, leg_ref, tend_ref):
    low = lax.broadcasted_iota(jnp.int32, (16, 128), 1) < 64
    hemispheres = ([], [])
    for side in range(2):
        for t in range(TRAJ):
            for level in range(FIELDS // 2):
                lane = FULL + 128 * level
                a = get(4 * t + 2 * side, lane).astype(F32)
                b = get(4 * t + 2 * side + 1, lane).astype(F32)
                last = (
                    jnp.where(low, a, pltpu.roll(b, 64, 1)),
                    jnp.where(low, pltpu.roll(a, 64, 1), b),
                )
                for h in range(2):
                    f = 2 * level + h
                    hemispheres[side].append(
                        jnp.concatenate(
                            [
                                get(4 * t + 2 * side, 128 * f).astype(F32),
                                get(4 * t + 2 * side + 1, 128 * f).astype(F32),
                                last[h],
                            ],
                            axis=1,
                        )
                    )
    north = jnp.stack(hemispheres[0])
    south = jnp.stack(hemispheres[1])
    upper = lax.broadcasted_iota(jnp.int32, (TRAJ * FIELDS, 8, NHALF), 1) < 4
    row8, _ = row_col(8, WIDTH)
    odd = ((row8 & 1) == 1)[None]
    sums = []
    for k in range(GROUP):
        rows = slice(8 * (k // 2), 8 * (k // 2) + 8)
        n, s = north[:, rows], south[:, rows]
        lhs = jnp.where(upper, n, swap4(s)) if k % 2 == 0 else jnp.where(upper, swap4(n), s)
        lhs = lhs.reshape(8 * TRAJ * FIELDS, NHALF).astype(BF16)
        dots = lax.dot_general(
            lhs, leg_ref[k], (((1,), (1,)), ((), ())), preferred_element_type=F32
        ).reshape(TRAJ * FIELDS, 8, WIDTH)
        dots = dots * sign_mask(first_pair + group * GROUP + k)[None]
        dots = dots + pltpu.roll(dots, 4, 1)
        sums.append(dots + pltpu.roll(dots, 2, 1))
    place = (row8 & 3)[None]
    here = (row8 >> 2) == (group & 1)
    for part in range(2):
        mixed = None
        for k in range(GROUP):
            turned = pltpu.roll(sums[k], 1, 1)
            every = jnp.where(odd, turned, sums[k]) if part == 0 else jnp.where(odd, sums[k], turned)
            mixed = every if k == 0 else jnp.where(place == k, every, mixed)
        for i in range(TRAJ * FIELDS):
            slot = tend_ref.at[2 * i + part, group >> 1]
            slot[...] = jnp.where(here, mixed[i], slot[...])


def semi_implicit(first_pair, x_ref, tend_ref, grav_ref, stab_ref, out_ref):
    g = [[grav_ref[a, b] for b in range(2)] for a in range(2)]
    s = [[stab_ref[a, b] for b in range(2)] for a in range(2)]
    k = [[g[a][0] * s[0][b] + g[a][1] * s[1][b] for b in range(2)] for a in range(2)]
    for tile in range(3):
        count = min(8, LOCAL - 8 * tile)
        row, col = row_col(count, WIDTH)
        pair = row + (first_pair + 8 * tile)
        leading = col < NW - pair
        degree = jnp.where(leading, col + pair, (NW - 1 - pair) + col - (NW - pair))
        lam = WAVE_SCALE * (degree * (degree + 1)).astype(F32) / float(NW * NW)
        damp = 1.0 / (1.0 + DIFFUSION * lam * lam)
        coupling = DT * DT * lam
        diag = [1.0 + coupling * k[a][a] for a in range(2)]
        cross = [coupling * k[0][1], coupling * k[1][0]]
        inverse = 1.0 / (diag[0] * diag[1] - cross[0] * cross[1])
        rows = slice(8 * tile, 8 * tile + count)

        def one(t, _):
            for part in range(2):
                def moved(f):
                    c = 2 * f + part
                    return x_ref[t, c, rows, :] + DT * tend_ref[12 * t + c, tile, 0:count, :]

                for a in range(2):
                    out_ref[t, 2 * a + part, rows, :] = damp * moved(a)
                heat = [moved(4), moved(5)]
                right = [
                    moved(2 + a) + DT * lam * (g[a][0] * heat[0] + g[a][1] * heat[1])
                    for a in range(2)
                ]
                new = [
                    (diag[1] * right[0] - cross[0] * right[1]) * inverse,
                    (diag[0] * right[1] - cross[1] * right[0]) * inverse,
                ]
                for a in range(2):
                    out_ref[t, 4 + 2 * a + part, rows, :] = damp * new[a]
                    out_ref[t, 8 + 2 * a + part, rows, :] = damp * (
                        heat[a] - DT * (s[a][0] * new[0] + s[a][1] * new[1])
                    )
            return 0

        lax.fori_loop(0, TRAJ, one, 0)


def project_kernel(back_ref, leg_ref, x_ref, grav_ref, stab_ref, out_ref, tend_ref):
    group = pl.program_id(0)
    first_pair = lax.axis_index("space") * LOCAL

    def get(block, lane):
        return back_ref[block, :, lane : lane + 128]

    project_group(group, first_pair, get, leg_ref, tend_ref)

    @pl.when(group == GROUPS - 1)
    def _():
        semi_implicit(first_pair, x_ref, tend_ref, grav_ref, stab_ref, out_ref)


def resident(shape):
    return pl.BlockSpec(shape, lambda *_: (0,) * len(shape))


STATE = (TRAJ, 2 * FIELDS, LOCAL, WIDTH)
LEG_BLOCK = pl.BlockSpec((GROUP, WIDTH, NHALF), lambda g: (g, 0, 0))
BAND_BLOCK = pl.BlockSpec((SPACE, 16, LANES), lambda g: (0, g, 0))
PARAMS = pltpu.CompilerParams(vmem_limit_bytes=56 * 1024 * 1024)


def to_fourier(state, legendre):
    return pl.pallas_call(
        legendre_kernel,
        grid=(GROUPS,),
        in_specs=[resident(STATE), LEG_BLOCK],
        out_specs=BAND_BLOCK,
        out_shape=jax.ShapeDtypeStruct((SPACE, ROWS, LANES), BF16),
        compiler_params=PARAMS,
        name="legendre",
    )(state, legendre)


def on_grid(fourier, sin_lat):
    tall, wide = zonal_tables()
    return pl.pallas_call(
        grid_kernel,
        out_shape=jax.ShapeDtypeStruct((4 * PAIRS, LANES), BF16),
        scratch_shapes=[pltpu.VMEM((NLON, LANES), BF16)],
        compiler_params=PARAMS,
        name="on_grid",
    )(fourier, jnp.asarray(tall), jnp.asarray(wide), sin_lat.reshape(1, NHALF))


def to_spectral(back, legendre, state, gravity, stability):
    smem = pl.BlockSpec(memory_space=pltpu.SMEM)
    return pl.pallas_call(
        project_kernel,
        grid=(GROUPS,),
        in_specs=[BAND_BLOCK, LEG_BLOCK, resident(STATE), smem, smem],
        out_specs=resident(STATE),
        out_shape=jax.ShapeDtypeStruct(STATE, F32),
        scratch_shapes=[pltpu.VMEM((TRAJ * 2 * FIELDS, 3, 8, WIDTH), F32)],
        compiler_params=PARAMS,
        name="project",
    )(back, legendre, state, gravity, stability)


def with_clones(state, clones):
    me = lax.axis_index("member")
    killed, source = clones[:, 0], clones[:, 1]
    picked = state[source % TRAJ]
    mine = (source // TRAJ == me)[:, None, None, None]
    received = lax.psum(jnp.where(mine, picked, 0.0), "member")
    rows = me * TRAJ + jnp.arange(TRAJ, dtype=jnp.int32)
    for entry in range(clones.shape[0]):
        here = (rows == killed[entry])[:, None, None, None]
        state = jnp.where(here, received[entry][None], state)
    return state


def exchange(blocks):
    return lax.all_to_all(blocks, "space", split_axis=0, concat_axis=0, tiled=True)


def shards(spectra, legendre, sin_lat, gravity, stability, clones):
    state = with_clones(spectra, clones)
    fourier = exchange(to_fourier(state, legendre))
    weighted = on_grid(fourier.reshape(SPACE * ROWS, LANES), sin_lat)
    back = exchange(weighted.reshape(SPACE, ROWS, LANES))
    return to_spectral(back, legendre, state, gravity, stability)


def solution(mesh):
    placed = (P("member", None, "space", None), P("space", None, None), P(), P(), P(), P())
    return jax.shard_map(
        shards,
        mesh=mesh,
        in_specs=placed,
        out_specs=P("member", None, "space", None),
        check_vma=False,
    )
```

time: 723 us -> 249 us (0.34)
  the two profiles are of different devices: /device:TPU:1 before, /device:TPU:6 now
where the time goes in v1:
time: 249 us; the launch traced here: 248 us
  waiting for transfers between devices  112 us (45%)
  blocking collectives  42.8 us (17%)
  Pallas kernels  39.2 us (16%)
  local copies, waits for them, and re-layouts  24.7 us (10%)
  between operations  13.5 us (5%)
  other arithmetic  8.78 us (4%)
  starting transfers between devices  7.11 us (3%)
    psum x1, waiting for transfers between devices, with_clones(): received = lax.psum(jnp.where(mine, picked, 0.0), 'member')  65.1 us
    all_to_all x1, waiting for transfers between devices, exchange(): lax.all_to_all(blocks, 'space', split_axis=0, concat_axis=0, tiled=True)  46.8 us
    all_to_all x1, blocking collectives, exchange(): lax.all_to_all(blocks, 'space', split_axis=0, concat_axis=0, tiled=True)  42.8 us
    pallas_call x1, Pallas kernels, on_grid(): pl.pallas_call(grid_kernel, out_shape=jax.ShapeDtypeStruct((4 * PAIRS, LA...  16.3 us
    pallas_call x1, Pallas kernels, to_spectral(): pl.pallas_call(project_kernel, grid=(GROUPS,), in_specs=[BAND_BLOCK, LEG_...  13.2 us
    pallas_call x1, Pallas kernels, to_fourier(): pl.pallas_call(legendre_kernel, grid=(GROUPS,), in_specs=[resident(STATE)...  9.77 us
    slice x1, local copies, waits for them, and re-layouts, with_clones(): state = jnp.where(here, received[entry][None], state)  8.09 us
    all_to_all x1, starting transfers between devices, exchange(): lax.all_to_all(blocks, 'space', split_axis=0, concat_axis=0, tiled=True)  7.11 us
  transfers between devices with their start and end apart: 2, of which 2 were waited for; matrix products, arithmetic and copies ran while one was open for 1% of the time, Pallas kernels for 0%

profile of v1, /device:TPU:6, one launch (start us, length us, event | category | flops | bytes accessed | tf_op | source)
XLA Modules:
  0.0 248.0 jit_solution(10448681969748702061)
XLA Ops:
  6.5 0.0 all-reduce.2.cloned.1.call-start
  6.5 0.7 fusion.4
  7.2 0.7 fusion.5
  7.9 6.4 %gather_fusion = f32[4,12,20,641]{3,0,2,1:T(4,128)S(1)} fusion(f32[4,12,20,641]{3,0,2,1:T(4,128)} %param.8, s32[1024]{0:T(1024)S(1)} %pad_clamp_fusion), kind=kCustom, calls=%fused_computation | custom fusion | bytes 4922896 | tf_op jit(solution)/shard_map/gather | solution.py:340
  14.3 0.0 copy-start.2
  14.4 2.4 broadcast_select_fusion
  16.8 0.0 all-reduce.2.cloned.1.call-update
  16.8 0.0 copy-done.2
  16.8 0.7 fusion.11
  17.5 1.3 fusion.8
  18.8 1.1 fusion.6
  19.9 65.1 %all-reduce.2.cloned.1.call-done = f32[4,12,20,641]{3,0,2,1:T(4,128)} async-done(((f32[4,12,20,641]{3,0,2,1:T(4,128)}), f32[4,12,20,641]{3,0,2,1:T(4,128)}) %all-reduce.2.cloned.1.call-update) | async-done | bytes 2461456 | tf_op jit(solution)/shard_map/psum | solution.py:342
  85.1 8.1 %fusion.10 = (f32[1,12,20,641]{3,0,2,1:T(1,128)S(1)}, f32[1,12,20,641]{3,0,2,1:T(1,128)S(1)}, f32[1,12,20,641]{3,0,2,1:T(1,128)S(1)}, f32[1,12,20,641]{3,0,2,1:T(1,128)S(1)}) fusion(f32[4,12,20,641]{3,0,2,1:T(4,128)} %all-reduce.2.cloned.1.call-done), kind=kLoop, calls=%fused_computation.28 | loop fusion | bytes 4922880 | tf_op jit(solution)/shard_map/slice | solution.py:346
  93.2 0.0 copy-start
  93.2 0.1 copy_bitcast_fusion.2
  93.3 0.2 copy_bitcast_fusion
  93.5 1.5 copy-done
  95.0 2.5 %fusion.2.x_ref = f32[4,12,20,641]{3,2,1,0:T(8,128)} fusion(f32[4,12,20,641]{3,0,2,1:T(4,128)S(1)} %copy-done, f32[12,20,641]{2,1,0:T(8,128)S(1)} %get-tuple-element.13, f32[12,20,641]{2,1,0:T(8,128)S(1)} %get-tuple-element.14, f32[12,20,641]{2,1,0:T(8,128)S(1)} %get-tuple-element.15, f32[12,20,641]{2,1,0:T(8,128)S(1)} %get-tuple-element.16, ...), kind=kLoop, calls=%fused_computation.4 | loop fusion | flops 2461440 | bytes 7384336 | tf_op jit(solution)/shard_map/jit(_where)/select_n | solution.py:346
  97.5 9.8 %legendre.1 = bf16[16,80,1152]{2,1,0:T(8,128)(2,1)} custom-call(f32[4,12,20,641]{3,2,1,0:T(8,128)} %fusion.2.x_ref, bf16[20,641,384]{2,1,0:T(8,128)(2,1)} %leg_ref.3), custom_call_target="tpu_custom_call" | custom-call | tf_op jit(solution)/shard_map/legendre/pallas_call | solution.py:301
  107.3 0.0 copy-start.3
  107.3 7.1 %all-to-all-start = ((bf16[16,80,1152]{2,1,0:T(8,128)(2,1)}), bf16[16,80,1152]{2,1,0:T(8,128)(2,1)S(1)}, u32[]{:S(2)}, u32[]{:S(2)}) async-start(bf16[16,80,1152]{2,1,0:T(8,128)(2,1)} %legendre.1), calls=%async_computation | async-start | bytes 5898240 | tf_op jit(solution)/shard_map/all_to_all | solution.py:351
  114.4 0.0 copy-done.3
  114.4 0.6 reshape.61.sin_ref
  115.0 46.8 %all-to-all-done = bf16[16,80,1152]{2,1,0:T(8,128)(2,1)S(1)} async-done(((bf16[16,80,1152]{2,1,0:T(8,128)(2,1)}), bf16[16,80,1152]{2,1,0:T(8,128)(2,1)S(1)}, u32[]{:S(2)}, u32[]{:S(2)}) %all-to-all-start) | async-done | bytes 2949152 | tf_op jit(solution)/shard_map/all_to_all | solution.py:351
  161.8 0.0 copy-start.1
  161.8 1.6 copy-done.1
  163.4 16.3 %on_grid.1 = bf16[1280,1152]{1,0:T(8,128)(2,1)} custom-call(bf16[1280,1152]{1,0:T(8,128)(2,1)} %bitcast.26, bf16[1280,1280]{1,0:T(8,128)(2,1)} %constant.42.clone.tall_ref, bf16[1280,1280]{1,0:T(8,128)(2,1)} %constant.43.clone.wide_ref, f32[1,384]{1,0:T(1,128)} %reshape.61.sin_ref), custom_call_target="tpu_custom_call" | custom-call | tf_op jit(solution)/shard_map/on_grid/pallas_call | solution.py:314
  179.7 42.8 %all_to_all.10.back_ref = bf16[16,80,1152]{2,1,0:T(8,128)(2,1)} all-to-all(bf16[16,80,1152]{2,1,0:T(8,128)(2,1)} %bitcast.27), channel_id=1, replica_groups=mesh['member'=8,'space'=16] {'space'}, dimensions={0} | all-to-all | bytes 5898240 | tf_op jit(solution)/shard_map/all_to_all | solution.py:351
  222.5 13.2 %project.1 = f32[4,12,20,641]{3,2,1,0:T(8,128)} custom-call(bf16[16,80,1152]{2,1,0:T(8,128)(2,1)} %all_to_all.10.back_ref, bf16[20,641,384]{2,1,0:T(8,128)(2,1)} %leg_ref.3, f32[4,12,20,641]{3,2,1,0:T(8,128)} %fusion.2.x_ref, f32[2,2]{1,0:T(2,128)} %grav_ref.1, f32[2,2]{1,0:T(2,128)} %stab_ref.1), custom_call_target="tpu_custom_call" | custom-call | tf_op jit(solution)/shard_map/project/pallas_call | solution.py:325
  235.7 5.5 %copy.12 = f32[4,12,20,641]{3,0,2,1:T(4,128)} copy(f32[4,12,20,641]{3,2,1,0:T(8,128)} %project.1) | data formatting | bytes 4922880 | tf_op jit(solution)/shard_map/project/pallas_call | solution.py:325
  (1 shorter events, 0.0 us)
Async XLA Ops:
  6.5 78.5 %all-reduce.2.cloned.1.call-start = ((), (), s32[]{:S(2)}) async-start(), calls=%async_computation.2 | async-start | bytes 5898240 | tf_op jit(solution)/shard_map/psum | solution.py:342
  14.3 2.5 copy-start.2
  93.2 1.8 copy-start
  107.3 7.1 %copy-start.3 = (f32[384]{0:T(512)S(1)}, f32[384]{0:T(512)}, u32[]{:S(2)}) copy-start(f32[384]{0:T(512)} %param.10) | copy-start | bytes 4612
  107.3 54.5 %all-to-all-start = ((bf16[16,80,1152]{2,1,0:T(8,128)(2,1)}), bf16[16,80,1152]{2,1,0:T(8,128)(2,1)S(1)}, u32[]{:S(2)}, u32[]{:S(2)}) async-start(bf16[16,80,1152]{2,1,0:T(8,128)(2,1)} %legendre.1), calls=%async_computation | async-start | bytes 5898240 | tf_op jit(solution)/shard_map/all_to_all | solution.py:351
  161.8 1.6 copy-start.1
Sparse Core Ops, SparseCore 0:
  16.9 68.0 all-reduce.1

commit v2 on v1

v2 whole, which is shorter than its diff:
```python
import functools
import math

import jax
import jax.numpy as jnp
import numpy as np
from jax import lax
from jax.experimental import pallas as pl
from jax.experimental.pallas import tpu as pltpu
from jax.sharding import PartitionSpec as P

NW = 640
WIDTH = NW + 1
NLON = 1280
NLAT = 768
NHALF = 384
PAIRS = 320
TRAJ = 4
FIELDS = 6
LOCAL = 20
SPACE = 16
GROUP = 4
GROUPS = LOCAL // GROUP
ROWS = 4 * LOCAL
FULL = 128 * FIELDS
LANES = FULL + 64 * FIELDS
PART = ((0, FULL), (FULL, LANES))
MEMBERS = 8
KILLED = 4
WIDE = 768
GROUPED = (GROUPS, TRAJ, 2 * FIELDS * GROUP, WIDE)
MESH = pl.DeviceIdType.MESH
DT = 0.25
WAVE_SCALE = 16.0
DIFFUSION = 0.02
F32 = jnp.float32
BF16 = jnp.bfloat16


@functools.cache
def zonal_tables():
    pair = np.arange(PAIRS)
    order = np.stack([pair, NW - 1 - pair], axis=1)
    phase = (order[:, :, None] * np.arange(NLON)) % NLON
    angle = phase * (2.0 * math.pi / NLON)
    table = np.stack([np.cos(angle), -np.sin(angle)], axis=2).reshape(4 * PAIRS, NLON)
    table = table.astype(jnp.bfloat16)
    return table, np.ascontiguousarray(table.T)


def row_col(rows, width):
    return (
        lax.broadcasted_iota(jnp.int32, (rows, width), 0),
        lax.broadcasted_iota(jnp.int32, (rows, width), 1),
    )


def sign_mask(pair):
    row, col = row_col(8, WIDTH)
    leading = (col < NW - pair).astype(jnp.int32)
    offset = jnp.where(leading == 1, col, col - (NW - pair))
    parity = (1 - 2 * (offset & 1)).astype(F32)
    sign = jnp.where(row >= 4, parity, 1.0)
    return jnp.where(((row >> 1) & 1) + leading == 1, sign, 0.0)


def swap4(value):
    return pltpu.roll(value, 4, 1)


def legendre_group(pair, xg_ref, leg_ref, put):
    row8, _ = row_col(8, WIDTH)
    odd = (row8 & 1) == 1
    results = []
    for k in range(GROUP):
        mask = sign_mask(pair + k)
        pieces = []
        for t in range(TRAJ):
            for f in range(FIELDS):
                real, imag = (
                    xg_ref[t, GROUP * c + k : GROUP * c + k + 1, 0:WIDTH] for c in (2 * f, 2 * f + 1)
                )
                pieces.append(jnp.where(odd, imag, real) * mask)
        lhs = jnp.concatenate(pieces, axis=0).astype(BF16)
        dots = jnp.dot(lhs, leg_ref[k], preferred_element_type=F32)
        results.append(dots.reshape(TRAJ * FIELDS, 8, NHALF))
    upper = lax.broadcasted_iota(jnp.int32, (TRAJ * FIELDS, 8, NHALF), 1) < 4
    hemispheres = ([], [])
    for k in range(0, GROUP, 2):
        first, second = results[k], results[k + 1]
        hemispheres[0].append(jnp.where(upper, first, swap4(second)))
        hemispheres[1].append(jnp.where(upper, swap4(first), second))
    low = lax.broadcasted_iota(jnp.int32, (16, 128), 1) < 64
    for side in range(2):
        one, two = hemispheres[side]
        for t in range(TRAJ):
            for level in range(FIELDS // 2):
                tiles = []
                for f in (2 * level, 2 * level + 1):
                    tile = jnp.concatenate([one[t * FIELDS + f], two[t * FIELDS + f]], axis=0)
                    put(4 * t + 2 * side, 128 * f, tile[:, 0:128].astype(BF16))
                    put(4 * t + 2 * side + 1, 128 * f, tile[:, 128:256].astype(BF16))
                    tiles.append(tile[:, 256:384])
                a, b = tiles
                lane = FULL + 128 * level
                put(4 * t + 2 * side, lane, jnp.where(low, a, pltpu.roll(b, 64, 1)).astype(BF16))
                put(
                    4 * t + 2 * side + 1, lane, jnp.where(low, pltpu.roll(a, 64, 1), b).astype(BF16)
                )


def latitude_rows(sin_ref, place):
    low = lax.broadcasted_iota(jnp.int32, (1, 128), 1) < 64
    zero, one, two = (sin_ref[:, 128 * i : 128 * i + 128] for i in range(3))
    swapped = pltpu.roll(two, 64, 1)
    second = (place & 1) == 1
    sign = jnp.where((place & 3) >= 2, -1.0, 1.0).astype(F32)
    full = jnp.where(second, one, zero) * sign
    half = jnp.where(second, jnp.where(low, swapped, two), jnp.where(low, two, swapped)) * sign
    return full, half


def forcing_of(spin, spread, heat, heat_swapped, coriolis):
    spun = spin + coriolis
    return (
        -spun * spread,
        spun * spin - 0.5 * spread * spread,
        -(heat + 0.5 * (heat + heat_swapped)) * spread,
    )


def grid_forward(part, sines, f_ref, wide_ref, forcing_ref):
    start, stop = PART[part]
    tile = 256

    def step(i, _):
        rows = pl.ds(pl.multiple_of(i * tile, tile), tile)
        sums = jnp.dot(wide_ref[rows, :], f_ref[:, start:stop], preferred_element_type=F32)
        sums = sums * (1.0 / NW)
        field = [sums[:, lane : lane + 128] for lane in range(0, stop - start, 128)]
        if part == 0:
            sets = [(field[a], field[2 + a], field[4 + a], field[5 - a]) for a in range(2)]
        else:
            sets = [(*field, pltpu.roll(field[2], 64, 1))]
        for a, fields in enumerate(sets):
            for g, made in enumerate(forcing_of(*fields, 2.0 * sines)):
                lane = start + 128 * (len(sets) * g + a)
                forcing_ref[rows, lane : lane + 128] = made.astype(BF16)
        return 0

    lax.fori_loop(0, NLON // tile, step, 0)


def grid_backward(part, sines, rows, forcing_ref, tall_ref, out_ref):
    start, stop = PART[part]
    weights = math.pi * jnp.sqrt(1.0 - sines * sines) / NLAT
    weights = jnp.concatenate([weights] * ((stop - start) // 128), axis=1)
    sums = jnp.dot(tall_ref[rows, :], forcing_ref[:, start:stop], preferred_element_type=F32)
    out_ref[rows, start:stop] = (sums * weights).astype(BF16)


def spread(axis, count, body):
    me = lax.axis_index(axis)

    def one(d, _):
        body(lax.rem(me + d, count))
        return 0

    lax.fori_loop(1, count, one, 0)


def main_kernel(
    clones_ref,
    x_ref,
    leg_any,
    tall_any,
    wide_any,
    sin_ref,
    back_ref,
    state_ref,
    leg_ref,
    tall_ref,
    wide_ref,
    xg_ref,
    hand_ref,
    landed_ref,
    shared_ref,
    send_ref,
    fourier_ref,
    forcing_ref,
    give_ref,
    leg_sem,
    table_sem,
    state_sem,
    own_sem,
    rs_send,
    rs_recv,
    ag_send,
    ag_recv,
    out_send,
    out_recv,
    half_send,
    half_recv,
    back_send,
    back_recv,
):
    member = lax.axis_index("member")
    place = lax.axis_index("space")
    sines = latitude_rows(sin_ref, place)
    leg_copies = []
    for g in range(GROUPS):
        some = pl.ds(g * GROUP, GROUP)
        leg_copies.append(
            pltpu.make_async_copy(leg_any.at[some], leg_ref.at[some], leg_sem.at[g])
        )
        leg_copies[-1].start()
    wide_copy = pltpu.make_async_copy(wide_any, wide_ref, table_sem.at[0])
    tall_copy = pltpu.make_async_copy(tall_any, tall_ref, table_sem.at[1])
    wide_copy.start()
    tall_copy.start()

    barrier = pltpu.get_barrier_semaphore()
    spread(
        "space",
        SPACE,
        lambda peer: pl.semaphore_signal(
            barrier, inc=1, device_id={"space": peer}, device_id_type=MESH
        ),
    )
    spread(
        "member",
        MEMBERS,
        lambda peer: pl.semaphore_signal(
            barrier, inc=1, device_id={"member": peer}, device_id_type=MESH
        ),
    )

    def scatter(q, g, peer, source):
        return pltpu.make_async_remote_copy(
            src_ref=hand_ref.at[q, g, peer],
            dst_ref=landed_ref.at[q, g, source],
            send_sem=rs_send.at[q, g, peer],
            recv_sem=rs_recv.at[q, g, source],
            device_id={"member": peer},
            device_id_type=MESH,
        )

    def gather(q, g, peer, source):
        return pltpu.make_async_remote_copy(
            src_ref=shared_ref.at[q, g, source],
            dst_ref=shared_ref.at[q, g, source],
            send_sem=ag_send.at[q, g, peer],
            recv_sem=ag_recv.at[q, g, source],
            device_id={"member": peer},
            device_id_type=MESH,
        )

    def regroup(g):
        some = slice(g * GROUP, g * GROUP + GROUP)
        for t in range(TRAJ):
            rows = jnp.concatenate([x_ref[t, c, some, :] for c in range(2 * FIELDS)], axis=0)
            xg_ref[g, t, :, 0:WIDTH] = rows
            xg_ref[g, t, :, NW:WIDE] = jnp.where(
                lax.broadcasted_iota(jnp.int32, (48, 128), 1) < 1, rows[:, NW:WIDTH], 0.0
            )

    def offer(q, g):
        for entry in range(KILLED):
            source = clones_ref[entry, 1]
            value = xg_ref[g, source & (TRAJ - 1)]
            high = value.astype(BF16)
            value = high if q == 0 else (value - high.astype(F32)).astype(BF16)
            value = jnp.where((source >> 2) == member, value.astype(F32), 0.0).astype(BF16)
            hand_ref[q, g, 2 * entry] = value[:, 0 : WIDE // 2]
            hand_ref[q, g, 2 * entry + 1] = value[:, WIDE // 2 : WIDE]
        spread("member", MEMBERS, lambda peer: scatter(q, g, peer, member).start())

    def settle(q, g):
        spread("member", MEMBERS, lambda peer: scatter(q, g, peer, peer).wait_recv())

        def add(d, total):
            return total + landed_ref[q, g, lax.rem(member + d, MEMBERS)].astype(F32)

        total = lax.fori_loop(1, MEMBERS, add, hand_ref[q, g, member].astype(F32))
        shared_ref[q, g, member] = total.astype(BF16)
        spread("member", MEMBERS, lambda peer: gather(q, g, peer, member).start())

    def arrived(q, g):
        spread("member", MEMBERS, lambda peer: gather(q, g, peer, peer).wait_recv())

    def adopt(g, parts):
        for entry in range(KILLED):
            value = None
            for q in range(parts):
                piece = jnp.concatenate(
                    [shared_ref[q, g, 2 * entry], shared_ref[q, g, 2 * entry + 1]], axis=1
                ).astype(F32)
                value = piece if value is None else value + piece
            for t in range(TRAJ):
                killed = clones_ref[entry, 0] == member * TRAJ + t
                xg_ref[g, t] = jnp.where(killed, value, xg_ref[g, t])

    def outward(g, peer, source):
        lanes = pl.ds(0, FULL)
        return pltpu.make_async_remote_copy(
            src_ref=send_ref.at[peer, pl.ds(g * 16, 16), lanes],
            dst_ref=fourier_ref.at[pl.ds(source * ROWS + g * 16, 16), lanes],
            send_sem=out_send.at[g, peer],
            recv_sem=out_recv.at[g, source],
            device_id={"space": peer},
            device_id_type=MESH,
        )

    def outward_half(peer, source):
        lanes = pl.ds(FULL, LANES - FULL)
        return pltpu.make_async_remote_copy(
            src_ref=send_ref.at[peer, :, lanes],
            dst_ref=fourier_ref.at[pl.ds(source * ROWS, ROWS), lanes],
            send_sem=half_send.at[peer],
            recv_sem=half_recv.at[source],
            device_id={"space": peer},
            device_id_type=MESH,
        )

    def homeward(part, peer, source):
        start, stop = PART[part]
        lanes = pl.ds(start, stop - start)
        return pltpu.make_async_remote_copy(
            src_ref=give_ref.at[pl.ds(peer * ROWS, ROWS), lanes],
            dst_ref=back_ref.at[source, :, lanes],
            send_sem=back_send.at[part, peer],
            recv_sem=back_recv.at[part, source],
            device_id={"space": peer},
            device_id_type=MESH,
        )

    for g in range(GROUPS):
        regroup(g)
        if g == 0:
            pl.semaphore_wait(barrier, SPACE + MEMBERS - 2)
        offer(0, g)
    settle(0, 0)

    def legendre_step(g, _):
        @pl.when(g + 1 < GROUPS)
        def _():
            settle(0, g + 1)

        arrived(0, g)
        adopt(g, 1)
        some = pl.ds(g * GROUP, GROUP)
        pltpu.make_async_copy(leg_any.at[some], leg_ref.at[some], leg_sem.at[g]).wait()

        def put(block, lane, value):
            send_ref[block, pl.ds(pl.multiple_of(g * 16, 16), 16), lane : lane + 128] = value

        legendre_group(
            place * LOCAL + g * GROUP, xg_ref.at[g], leg_ref.at[pl.ds(g * GROUP, GROUP)], put
        )
        spread("space", SPACE, lambda peer: outward(g, peer, place).start())
        return 0

    lax.fori_loop(0, GROUPS, legendre_step, 0)
    own_out = pltpu.make_async_copy(
        send_ref.at[place], fourier_ref.at[pl.ds(place * ROWS, ROWS)], own_sem.at[0]
    )
    own_out.start()
    spread("space", SPACE, lambda peer: outward_half(peer, place).start())

    def each_group(body):
        def one(g, _):
            body(g)
            return 0

        lax.fori_loop(0, GROUPS, one, 0)

    each_group(lambda g: offer(1, g))
    wide_copy.wait()
    tall_copy.wait()
    own_out.wait()
    each_group(
        lambda g: spread("space", SPACE, lambda peer: outward(g, peer, peer).wait_recv())
    )
    quarter = 4 * ROWS
    for part in range(2):
        if part == 1:
            spread("space", SPACE, lambda peer: outward_half(peer, peer).wait_recv())
        grid_forward(part, sines[part], fourier_ref, wide_ref, forcing_ref)

        def backward(i, _, part=part):
            block = lax.rem((place >> 2) + i, 4)
            rows = pl.ds(pl.multiple_of(block * quarter, quarter), quarter)
            grid_backward(part, sines[part], rows, forcing_ref, tall_ref, give_ref)

            def one(j, _):
                peer = block * 4 + lax.rem((place & 3) + j, 4)

                @pl.when(peer != place)
                def _():
                    homeward(part, peer, place).start()

                return 0

            lax.fori_loop(0, 4, one, 0)
            return 0

        lax.fori_loop(0, 4, backward, 0)
        if part == 0:
            each_group(lambda g: settle(1, g))
    own_back = pltpu.make_async_copy(
        give_ref.at[pl.ds(place * ROWS, ROWS)], back_ref.at[place], own_sem.at[1]
    )
    own_back.start()

    def complete(g):
        arrived(1, g)
        adopt(g, 2)

    each_group(complete)
    state_copy = pltpu.make_async_copy(xg_ref, state_ref, state_sem)
    state_copy.start()
    for q in range(2):
        each_group(
            lambda g: spread("member", MEMBERS, lambda peer: scatter(q, g, peer, peer).wait_send())
        )
        each_group(
            lambda g: spread("member", MEMBERS, lambda peer: gather(q, g, peer, member).wait_send())
        )
    each_group(
        lambda g: spread("space", SPACE, lambda peer: outward(g, peer, place).wait_send())
    )
    spread("space", SPACE, lambda peer: outward_half(peer, place).wait_send())
    for part in range(2):
        spread("space", SPACE, lambda peer: homeward(part, peer, place).wait_send())
        spread("space", SPACE, lambda peer: homeward(part, peer, peer).wait_recv())
    own_back.wait()
    state_copy.wait()


def project_group(group, first_pair, get, leg_ref):
    low = lax.broadcasted_iota(jnp.int32, (16, 128), 1) < 64
    hemispheres = ([], [])
    for side in range(2):
        for t in range(TRAJ):
            for level in range(FIELDS // 2):
                lane = FULL + 128 * level
                a = get(4 * t + 2 * side, lane).astype(F32)
                b = get(4 * t + 2 * side + 1, lane).astype(F32)
                last = (
                    jnp.where(low, a, pltpu.roll(b, 64, 1)),
                    jnp.where(low, pltpu.roll(a, 64, 1), b),
                )
                for h in range(2):
                    f = 2 * level + h
                    hemispheres[side].append(
                        jnp.concatenate(
                            [
                                get(4 * t + 2 * side, 128 * f).astype(F32),
                                get(4 * t + 2 * side + 1, 128 * f).astype(F32),
                                last[h],
                            ],
                            axis=1,
                        )
                    )
    north = jnp.stack(hemispheres[0])
    south = jnp.stack(hemispheres[1])
    upper = lax.broadcasted_iota(jnp.int32, (TRAJ * FIELDS, 8, NHALF), 1) < 4
    row8, _ = row_col(8, WIDTH)
    odd = ((row8 & 1) == 1)[None]
    sums = []
    for k in range(GROUP):
        rows = slice(8 * (k // 2), 8 * (k // 2) + 8)
        n, s = north[:, rows], south[:, rows]
        lhs = jnp.where(upper, n, swap4(s)) if k % 2 == 0 else jnp.where(upper, swap4(n), s)
        lhs = lhs.reshape(8 * TRAJ * FIELDS, NHALF).astype(BF16)
        dots = lax.dot_general(
            lhs, leg_ref[k], (((1,), (1,)), ((), ())), preferred_element_type=F32
        ).reshape(TRAJ * FIELDS, 8, WIDTH)
        dots = dots * sign_mask(first_pair + group * GROUP + k)[None]
        dots = dots + pltpu.roll(dots, 4, 1)
        sums.append(dots + pltpu.roll(dots, 2, 1))
    place = (row8 & 3)[None]
    upper = (row8 < 4)[None]
    mixed = []
    for part in range(2):
        some = None
        for k in range(GROUP):
            turned = pltpu.roll(sums[k], 1, 1)
            every = jnp.where(odd, turned, sums[k]) if part == 0 else jnp.where(odd, sums[k], turned)
            some = every if k == 0 else jnp.where(place == k, every, some)
        mixed.append(some)
    return jnp.where(upper, mixed[0], mixed[1])


def semi_implicit(pair, group, state_ref, tend, grav_ref, stab_ref, new_ref):
    g = [[grav_ref[a, b] for b in range(2)] for a in range(2)]
    s = [[stab_ref[a, b] for b in range(2)] for a in range(2)]
    k = [[g[a][0] * s[0][b] + g[a][1] * s[1][b] for b in range(2)] for a in range(2)]
    row, col = row_col(8, WIDTH)
    pair = pair + (row & 3)
    degree = jnp.where(col < NW - pair, col + pair, (NW - 1 - pair) + col - (NW - pair))
    lam = WAVE_SCALE * (degree * (degree + 1)).astype(F32) / float(NW * NW)
    damp = 1.0 / (1.0 + DIFFUSION * lam * lam)
    coupling = DT * DT * lam
    diag = [1.0 + coupling * k[a][a] for a in range(2)]
    cross = [coupling * k[0][1], coupling * k[1][0]]
    inverse = 1.0 / (diag[0] * diag[1] - cross[0] * cross[1])
    upper = row < 4
    here = (row >> 2) == (group & 1)
    for t in range(TRAJ):

        def moved(f):
            return state_ref[0, t, 8 * f : 8 * f + 8, 0:WIDTH] + DT * tend[t * FIELDS + f]

        def place(f, value):
            turned = pltpu.roll(value, 4, 0)
            for part in range(2):
                both = jnp.where(upper, turned, value) if part else jnp.where(upper, value, turned)
                slot = new_ref.at[2 * (t * FIELDS + f) + part, group >> 1]
                slot[...] = jnp.where(here, both, slot[...])

        for a in range(2):
            place(a, damp * moved(a))
        heat = [moved(4), moved(5)]
        right = [
            moved(2 + a) + DT * lam * (g[a][0] * heat[0] + g[a][1] * heat[1]) for a in range(2)
        ]
        new = [
            (diag[1] * right[0] - cross[0] * right[1]) * inverse,
            (diag[0] * right[1] - cross[1] * right[0]) * inverse,
        ]
        for a in range(2):
            place(2 + a, damp * new[a])
            place(4 + a, damp * (heat[a] - DT * (s[a][0] * new[0] + s[a][1] * new[1])))


def project_kernel(back_ref, leg_ref, state_ref, grav_ref, stab_ref, out_ref, new_ref):
    group = pl.program_id(0)
    first_pair = lax.axis_index("space") * LOCAL

    def get(block, lane):
        return back_ref[block, :, lane : lane + 128]

    tend = project_group(group, first_pair, get, leg_ref)
    semi_implicit(first_pair + group * GROUP, group, state_ref, tend, grav_ref, stab_ref, new_ref)

    @pl.when(group == GROUPS - 1)
    def _():
        def finish(t, _):
            for c in range(2 * FIELDS):
                for tile in range(3):
                    rows = min(8, LOCAL - 8 * tile)
                    value = new_ref[2 * FIELDS * t + c, tile, 0:rows, :]
                    out_ref[t, c, 8 * tile : 8 * tile + rows, :] = value
            return 0

        lax.fori_loop(0, TRAJ, finish, 0)


def resident(shape):
    return pl.BlockSpec(shape, lambda *_: (0,) * len(shape))


STATE = (TRAJ, 2 * FIELDS, LOCAL, WIDTH)
LEG_BLOCK = pl.BlockSpec((GROUP, WIDTH, NHALF), lambda g: (g, 0, 0))
BAND_BLOCK = pl.BlockSpec((SPACE, 16, LANES), lambda g: (0, g, 0))


def to_bands(spectra, legendre, sin_lat, clones):
    tall, wide = zonal_tables()
    anywhere = pl.BlockSpec(memory_space=pl.ANY)
    vmem = pl.BlockSpec(memory_space=pltpu.VMEM)
    smem = pl.BlockSpec(memory_space=pltpu.SMEM)
    dma = pltpu.SemaphoreType.DMA
    pieces = (2, GROUPS, MEMBERS, 2 * FIELDS * GROUP, WIDE // 2)
    band = (4 * PAIRS, LANES)
    return pl.pallas_call(
        main_kernel,
        in_specs=[smem, vmem, anywhere, anywhere, anywhere, vmem],
        out_specs=[anywhere, anywhere],
        out_shape=[
            jax.ShapeDtypeStruct((SPACE, ROWS, LANES), BF16),
            jax.ShapeDtypeStruct(GROUPED, F32),
        ],
        scratch_shapes=[
            pltpu.VMEM((LOCAL, WIDTH, NHALF), BF16),
            pltpu.VMEM((4 * PAIRS, NLON), BF16),
            pltpu.VMEM((NLON, 4 * PAIRS), BF16),
            pltpu.VMEM(GROUPED, F32),
            pltpu.VMEM(pieces, BF16),
            pltpu.VMEM(pieces, BF16),
            pltpu.VMEM(pieces, BF16),
            pltpu.VMEM((SPACE, ROWS, LANES), BF16),
            pltpu.VMEM(band, BF16),
            pltpu.VMEM(band, BF16),
            pltpu.VMEM(band, BF16),
            dma((GROUPS,)),
            dma((2,)),
            dma,
            dma((2,)),
            dma((2, GROUPS, MEMBERS)),
            dma((2, GROUPS, MEMBERS)),
            dma((2, GROUPS, MEMBERS)),
            dma((2, GROUPS, MEMBERS)),
            dma((GROUPS, SPACE)),
            dma((GROUPS, SPACE)),
            dma((SPACE,)),
            dma((SPACE,)),
            dma((2, SPACE)),
            dma((2, SPACE)),
        ],
        compiler_params=pltpu.CompilerParams(
            vmem_limit_bytes=60 * 1024 * 1024, collective_id=0, has_side_effects=True
        ),
        name="bands",
    )(clones, spectra, legendre, jnp.asarray(tall), jnp.asarray(wide), sin_lat.reshape(1, NHALF))


def to_spectral(back, legendre, state, gravity, stability):
    smem = pl.BlockSpec(memory_space=pltpu.SMEM)
    return pl.pallas_call(
        project_kernel,
        grid=(GROUPS,),
        in_specs=[
            BAND_BLOCK,
            LEG_BLOCK,
            pl.BlockSpec((1,) + GROUPED[1:], lambda g: (g, 0, 0, 0)),
            smem,
            smem,
        ],
        out_specs=resident(STATE),
        out_shape=jax.ShapeDtypeStruct(STATE, F32),
        scratch_shapes=[pltpu.VMEM((TRAJ * 2 * FIELDS, 3, 8, WIDTH), F32)],
        compiler_params=pltpu.CompilerParams(vmem_limit_bytes=56 * 1024 * 1024),
        name="project",
    )(back, legendre, state, gravity, stability)


def shards(spectra, legendre, sin_lat, gravity, stability, clones):
    back, state = to_bands(spectra, legendre, sin_lat, clones)
    return to_spectral(back, legendre, state, gravity, stability)


def solution(mesh):
    placed = (P("member", None, "space", None), P("space", None, None), P(), P(), P(), P())
    return jax.shard_map(
        shards,
        mesh=mesh,
        in_specs=placed,
        out_specs=P("member", None, "space", None),
        check_vma=False,
    )
```

time: 249 us -> 138 us (0.55)
  the two profiles are of different devices: /device:TPU:6 before, /device:TPU:1 now
where the time goes in v2:
time: 138 us; the launch traced here: 137 us
  Pallas kernels  124 us (90%)
  local copies, waits for them, and re-layouts  12.3 us (9%)
    pallas_call x1, Pallas kernels, to_bands(): pl.pallas_call(main_kernel, in_specs=[smem, vmem, anywhere, anywhere, any...  112 us
    pallas_call x1, Pallas kernels, to_spectral(): pl.pallas_call(project_kernel, grid=(GROUPS,), in_specs=[BAND_BLOCK, LEG_...  12.3 us
    unnamed x2, local copies, waits for them, and re-layouts  5.53 us
    pallas_call x1, local copies, waits for them, and re-layouts, to_spectral(): pl.pallas_call(project_kernel, grid=(GROUPS,), in_specs=[BAND_BLOCK, LEG_...  5.5 us

profile of v2, /device:TPU:1, one launch (start us, length us, event | category | flops | bytes accessed | tf_op | source)
XLA Modules:
  0.0 136.7 jit_solution(4186748164028275104)
XLA Ops:
  0.0 1.3 reshape.3.sin_ref
  1.3 1.3 copy.9.clones_ref
  2.6 4.2 %copy.10.x_ref = f32[4,12,20,641]{3,2,1,0:T(8,128)} copy(f32[4,12,20,641]{3,0,2,1:T(4,128)} %param.8) | data formatting | bytes 4922880 | tf_op args[0]
  6.8 112.1 %bands.1 = (bf16[16,80,1152]{2,1,0:T(8,128)(2,1)}, f32[5,4,48,768]{3,2,1,0:T(8,128)}) custom-call(s32[4,2]{1,0:T(4,128)} %copy.9.clones_ref, f32[4,12,20,641]{3,2,1,0:T(8,128)} %copy.10.x_ref, bf16[20,641,384]{2,1,0:T(8,128)(2,1)} %leg_ref.1, bf16[1280,1280]{1,0:T(8,128)(2,1)} %constant.4.clone.tall_any, bf16[1280,1280]{1,0:T(8,128)(2,1)} %constant.5.clone.wide_any, ...), custom_call_target="tpu_custom_call" | custom-call | tf_op jit(solution)/shard_map/bands/pallas_call | solution.py:577
  118.9 12.3 %project.1 = f32[4,12,20,641]{3,2,1,0:T(8,128)} custom-call(bf16[16,80,1152]{2,1,0:T(8,128)(2,1)} %get-tuple-element.7.back_ref, bf16[20,641,384]{2,1,0:T(8,128)(2,1)} %leg_ref.1, f32[5,4,48,768]{3,2,1,0:T(8,128)} %get-tuple-element.8.state_ref, f32[2,2]{1,0:T(2,128)} %grav_ref.1, f32[2,2]{1,0:T(2,128)} %stab_ref.1), custom_call_target="tpu_custom_call" | custom-call | tf_op jit(solution)/shard_map/project/pallas_call | solution.py:621
  131.2 5.5 %copy.11 = f32[4,12,20,641]{3,0,2,1:T(4,128)} copy(f32[4,12,20,641]{3,2,1,0:T(8,128)} %project.1) | data formatting | bytes 4922880 | tf_op jit(solution)/shard_map/project/pallas_call | solution.py:621

commit v3 on v2

--- a/solution.py
+++ b/solution.py
@@ -28,7 +28,8 @@
 MEMBERS = 8
 KILLED = 4
 WIDE = 768
-GROUPED = (GROUPS, TRAJ, 2 * FIELDS * GROUP, WIDE)
+GROUPED = (GROUPS, 2 * FIELDS, GROUP, TRAJ, WIDTH)
+MIX = 2 * FIELDS * GROUP
 MESH = pl.DeviceIdType.MESH
 DT = 0.25
 WAVE_SCALE = 16.0
@@ -68,7 +69,7 @@
     return pltpu.roll(value, 4, 1)
 
 
-def legendre_group(pair, xg_ref, leg_ref, put):
+def legendre_group(pair, now_ref, leg_ref, put):
     row8, _ = row_col(8, WIDTH)
     odd = (row8 & 1) == 1
     results = []
@@ -77,9 +78,8 @@
         pieces = []
         for t in range(TRAJ):
             for f in range(FIELDS):
-                real, imag = (
-                    xg_ref[t, GROUP * c + k : GROUP * c + k + 1, 0:WIDTH] for c in (2 * f, 2 * f + 1)
-                )
+                first = MIX * t + 2 * GROUP * f + k
+                real, imag = (now_ref[row : row + 1, 0:WIDTH] for row in (first, first + GROUP))
                 pieces.append(jnp.where(odd, imag, real) * mask)
         lhs = jnp.concatenate(pieces, axis=0).astype(BF16)
         dots = jnp.dot(lhs, leg_ref[k], preferred_element_type=F32)
@@ -159,6 +159,61 @@
     out_ref[rows, start:stop] = (sums * weights).astype(BF16)
 
 
+def one_hot(condition):
+    return jnp.where(condition, 1.0, 0.0).astype(BF16)
+
+
+def square(rows):
+    return row_col(rows, TRAJ * MIX)
+
+
+def select_rows(clones_ref, member):
+    row, col = square(MIX)
+    parts = []
+    for entry in range(KILLED):
+        source = clones_ref[1, entry]
+        wanted = jnp.where((source >> 2) == member, source & (TRAJ - 1), TRAJ)
+        parts.append(one_hot((row == (col >> 2)) & ((col & 3) == wanted)))
+    return jnp.concatenate(parts, axis=0)
+
+
+def entry_of(clones_ref, number):
+    found = KILLED
+    for entry in range(KILLED):
+        found = jnp.where(clones_ref[0, entry] == number, entry, found)
+    return found
+
+
+def entry_columns(col):
+    return sum((col >= MIX * i).astype(jnp.int32) for i in range(1, KILLED))
+
+
+def keep_and_put(clones_ref, member):
+    row, col = square(MIX)
+    entry = entry_columns(col)
+    keep, put = [], []
+    for t in range(TRAJ):
+        found = entry_of(clones_ref, member * TRAJ + t)
+        own = jnp.where(found == KILLED, t, TRAJ)
+        keep.append(one_hot((row == (col >> 2)) & ((col & 3) == own)))
+        put.append(one_hot((row == col - MIX * entry) & (entry == found)))
+    return jnp.concatenate(keep, axis=0), jnp.concatenate(put, axis=0)
+
+
+def by_trajectory(values, row):
+    mixed = values[0]
+    for t in range(1, TRAJ):
+        mixed = jnp.where(row == t, values[t], mixed)
+    return mixed
+
+
+def place_rows(clones_ref, member):
+    row, col = square(TRAJ * MIX)
+    entry = entry_columns(col)
+    found = [entry_of(clones_ref, member * TRAJ + t) for t in range(TRAJ)]
+    return one_hot((entry == by_trajectory(found, row & 3)) & ((row >> 2) == col - MIX * entry))
+
+
 def spread(axis, count, body):
     me = lax.axis_index(axis)
 
@@ -171,7 +226,7 @@
 
 def main_kernel(
     clones_ref,
-    x_ref,
+    x_any,
     leg_any,
     tall_any,
     wide_any,
@@ -182,6 +237,8 @@
     tall_ref,
     wide_ref,
     xg_ref,
+    half_ref,
+    now_ref,
     hand_ref,
     landed_ref,
     shared_ref,
@@ -189,6 +246,7 @@
     fourier_ref,
     forcing_ref,
     give_ref,
+    x_sem,
     leg_sem,
     table_sem,
     state_sem,
@@ -207,13 +265,18 @@
     member = lax.axis_index("member")
     place = lax.axis_index("space")
     sines = latitude_rows(sin_ref, place)
-    leg_copies = []
-    for g in range(GROUPS):
+
+    def x_copy(g):
         some = pl.ds(g * GROUP, GROUP)
-        leg_copies.append(
-            pltpu.make_async_copy(leg_any.at[some], leg_ref.at[some], leg_sem.at[g])
-        )
-        leg_copies[-1].start()
+        return pltpu.make_async_copy(x_any.at[:, some], xg_ref.at[g], x_sem.at[g])
+
+    def leg_copy(g):
+        some = pl.ds(g * GROUP, GROUP)
+        return pltpu.make_async_copy(leg_any.at[some], leg_ref.at[some], leg_sem.at[g])
+
+    for copy in (x_copy, leg_copy):
+        for g in range(GROUPS):
+            copy(g).start()
     wide_copy = pltpu.make_async_copy(wide_any, wide_ref, table_sem.at[0])
     tall_copy = pltpu.make_async_copy(tall_any, tall_ref, table_sem.at[1])
     wide_copy.start()
@@ -256,23 +319,25 @@
         )
 
     def regroup(g):
-        some = slice(g * GROUP, g * GROUP + GROUP)
-        for t in range(TRAJ):
-            rows = jnp.concatenate([x_ref[t, c, some, :] for c in range(2 * FIELDS)], axis=0)
-            xg_ref[g, t, :, 0:WIDTH] = rows
-            xg_ref[g, t, :, NW:WIDE] = jnp.where(
-                lax.broadcasted_iota(jnp.int32, (48, 128), 1) < 1, rows[:, NW:WIDTH], 0.0
-            )
+        rows = jnp.concatenate(
+            [xg_ref[g, c, p] for c in range(2 * FIELDS) for p in range(GROUP)], axis=0
+        )
+        _, lane = row_col(TRAJ * MIX, 128)
+        value = jnp.concatenate(
+            [rows[:, 0:NW], jnp.where(lane < 1, rows[:, NW:WIDTH], 0.0)], axis=1
+        )
+        high = value.astype(BF16)
+        half_ref[0, g] = high
+        half_ref[1, g] = (value - high.astype(F32)).astype(BF16)
+
+    selection = select_rows(clones_ref, member)
 
     def offer(q, g):
+        value = jnp.dot(selection, half_ref[q, g], preferred_element_type=F32).astype(BF16)
         for entry in range(KILLED):
-            source = clones_ref[entry, 1]
-            value = xg_ref[g, source & (TRAJ - 1)]
-            high = value.astype(BF16)
-            value = high if q == 0 else (value - high.astype(F32)).astype(BF16)
-            value = jnp.where((source >> 2) == member, value.astype(F32), 0.0).astype(BF16)
-            hand_ref[q, g, 2 * entry] = value[:, 0 : WIDE // 2]
-            hand_ref[q, g, 2 * entry + 1] = value[:, WIDE // 2 : WIDE]
+            rows = slice(MIX * entry, MIX * entry + MIX)
+            hand_ref[q, g, 2 * entry] = value[rows, 0 : WIDE // 2]
+            hand_ref[q, g, 2 * entry + 1] = value[rows, WIDE // 2 : WIDE]
         spread("member", MEMBERS, lambda peer: scatter(q, g, peer, member).start())
 
     def settle(q, g):
@@ -288,17 +353,14 @@
     def arrived(q, g):
         spread("member", MEMBERS, lambda peer: gather(q, g, peer, peer).wait_recv())
 
-    def adopt(g, parts):
-        for entry in range(KILLED):
-            value = None
-            for q in range(parts):
-                piece = jnp.concatenate(
-                    [shared_ref[q, g, 2 * entry], shared_ref[q, g, 2 * entry + 1]], axis=1
-                ).astype(F32)
-                value = piece if value is None else value + piece
-            for t in range(TRAJ):
-                killed = clones_ref[entry, 0] == member * TRAJ + t
-                xg_ref[g, t] = jnp.where(killed, value, xg_ref[g, t])
+    def received(q, g):
+        return jnp.concatenate(
+            [
+                jnp.concatenate([shared_ref[q, g, 2 * e], shared_ref[q, g, 2 * e + 1]], axis=1)
+                for e in range(KILLED)
+            ],
+            axis=0,
+        )
 
     def outward(g, peer, source):
         lanes = pl.ds(0, FULL)
@@ -334,11 +396,19 @@
             device_id_type=MESH,
         )
 
-    for g in range(GROUPS):
+    x_copy(0).wait()
+    regroup(0)
+    pl.semaphore_wait(barrier, SPACE + MEMBERS - 2)
+    offer(0, 0)
+
+    def rest(g, _):
+        x_copy(g).wait()
         regroup(g)
-        if g == 0:
-            pl.semaphore_wait(barrier, SPACE + MEMBERS - 2)
         offer(0, g)
+        return 0
+
+    lax.fori_loop(1, GROUPS, rest, 0)
+    keep, put_rows = keep_and_put(clones_ref, member)
     settle(0, 0)
 
     def legendre_step(g, _):
@@ -347,15 +417,15 @@
             settle(0, g + 1)
 
         arrived(0, g)
-        adopt(g, 1)
-        some = pl.ds(g * GROUP, GROUP)
-        pltpu.make_async_copy(leg_any.at[some], leg_ref.at[some], leg_sem.at[g]).wait()
+        now = jnp.dot(keep, half_ref[0, g], preferred_element_type=F32)
+        now_ref[...] = now + jnp.dot(put_rows, received(0, g), preferred_element_type=F32)
+        leg_copy(g).wait()
 
         def put(block, lane, value):
             send_ref[block, pl.ds(pl.multiple_of(g * 16, 16), 16), lane : lane + 128] = value
 
         legendre_group(
-            place * LOCAL + g * GROUP, xg_ref.at[g], leg_ref.at[pl.ds(g * GROUP, GROUP)], put
+            place * LOCAL + g * GROUP, now_ref, leg_ref.at[pl.ds(g * GROUP, GROUP)], put
         )
         spread("space", SPACE, lambda peer: outward(g, peer, place).start())
         return 0
@@ -412,9 +482,22 @@
     )
     own_back.start()
 
+    placing = place_rows(clones_ref, member)
+    row, _ = row_col(TRAJ, WIDTH)
+    killed = by_trajectory(
+        [entry_of(clones_ref, member * TRAJ + t) for t in range(TRAJ)], row
+    )
+
     def complete(g):
         arrived(1, g)
-        adopt(g, 2)
+        value = sum(
+            jnp.dot(placing, received(q, g), preferred_element_type=F32) for q in range(2)
+        )
+        for c in range(2 * FIELDS):
+            for p in range(GROUP):
+                first = (c * GROUP + p) * TRAJ
+                new = value[first : first + TRAJ, 0:WIDTH]
+                xg_ref[g, c, p] = jnp.where(killed < KILLED, new, xg_ref[g, c, p])
 
     each_group(complete)
     state_copy = pltpu.make_async_copy(xg_ref, state_ref, state_sem)
@@ -437,131 +520,99 @@
     state_copy.wait()
 
 
-def project_group(group, first_pair, get, leg_ref):
-    low = lax.broadcasted_iota(jnp.int32, (16, 128), 1) < 64
-    hemispheres = ([], [])
-    for side in range(2):
-        for t in range(TRAJ):
-            for level in range(FIELDS // 2):
-                lane = FULL + 128 * level
-                a = get(4 * t + 2 * side, lane).astype(F32)
-                b = get(4 * t + 2 * side + 1, lane).astype(F32)
-                last = (
-                    jnp.where(low, a, pltpu.roll(b, 64, 1)),
-                    jnp.where(low, pltpu.roll(a, 64, 1), b),
-                )
-                for h in range(2):
-                    f = 2 * level + h
-                    hemispheres[side].append(
-                        jnp.concatenate(
-                            [
-                                get(4 * t + 2 * side, 128 * f).astype(F32),
-                                get(4 * t + 2 * side + 1, 128 * f).astype(F32),
-                                last[h],
-                            ],
-                            axis=1,
-                        )
-                    )
-    north = jnp.stack(hemispheres[0])
-    south = jnp.stack(hemispheres[1])
-    upper = lax.broadcasted_iota(jnp.int32, (TRAJ * FIELDS, 8, NHALF), 1) < 4
-    row8, _ = row_col(8, WIDTH)
-    odd = ((row8 & 1) == 1)[None]
-    sums = []
-    for k in range(GROUP):
-        rows = slice(8 * (k // 2), 8 * (k // 2) + 8)
-        n, s = north[:, rows], south[:, rows]
-        lhs = jnp.where(upper, n, swap4(s)) if k % 2 == 0 else jnp.where(upper, swap4(n), s)
-        lhs = lhs.reshape(8 * TRAJ * FIELDS, NHALF).astype(BF16)
-        dots = lax.dot_general(
-            lhs, leg_ref[k], (((1,), (1,)), ((), ())), preferred_element_type=F32
-        ).reshape(TRAJ * FIELDS, 8, WIDTH)
-        dots = dots * sign_mask(first_pair + group * GROUP + k)[None]
-        dots = dots + pltpu.roll(dots, 4, 1)
-        sums.append(dots + pltpu.roll(dots, 2, 1))
-    place = (row8 & 3)[None]
-    upper = (row8 < 4)[None]
-    mixed = []
-    for part in range(2):
-        some = None
-        for k in range(GROUP):
-            turned = pltpu.roll(sums[k], 1, 1)
-            every = jnp.where(odd, turned, sums[k]) if part == 0 else jnp.where(odd, sums[k], turned)
-            some = every if k == 0 else jnp.where(place == k, every, some)
-        mixed.append(some)
-    return jnp.where(upper, mixed[0], mixed[1])
-
-
-def semi_implicit(pair, group, state_ref, tend, grav_ref, stab_ref, new_ref):
+def unmix():
+    row, col = row_col(128, 128)
+    t, half, side, part, pair = row & 3, (row >> 2) & 1, (row >> 3) & 1, (row >> 4) & 1, row >> 5
+    return one_hot(col == 32 * t + 16 * side + 4 * pair + 2 * half + part)
+
+
+def project_rows(back_ref):
+    low = lax.broadcasted_iota(jnp.int32, (128, 128), 1) < 64
+    order = unmix()
+
+    def column(odd, lane):
+        return jnp.concatenate(
+            [
+                back_ref[4 * t + 2 * side + odd, :, lane : lane + 128]
+                for t in range(TRAJ)
+                for side in range(2)
+            ],
+            axis=0,
+        )
+
+    fields = []
+    for level in range(FIELDS // 2):
+        lanes = [256 * level, 256 * level + 128, FULL + 128 * level]
+        mixed = jnp.concatenate([column(odd, lane) for lane in lanes for odd in range(2)], axis=1)
+        rows = jnp.dot(order, mixed, preferred_element_type=F32)
+        a, b = rows[:, 512:640], rows[:, 640:768]
+        last = (
+            jnp.where(low, a, pltpu.roll(b, 64, 1)),
+            jnp.where(low, pltpu.roll(a, 64, 1), b),
+        )
+        for h in range(2):
+            fields.append(
+                jnp.concatenate([rows[:, 256 * h : 256 * h + 256], last[h]], axis=1).astype(BF16)
+            )
+    return fields
+
+
+def project_kernel(back_ref, leg_ref, state_ref, grav_ref, stab_ref, out_ref):
     g = [[grav_ref[a, b] for b in range(2)] for a in range(2)]
     s = [[stab_ref[a, b] for b in range(2)] for a in range(2)]
-    k = [[g[a][0] * s[0][b] + g[a][1] * s[1][b] for b in range(2)] for a in range(2)]
-    row, col = row_col(8, WIDTH)
-    pair = pair + (row & 3)
-    degree = jnp.where(col < NW - pair, col + pair, (NW - 1 - pair) + col - (NW - pair))
-    lam = WAVE_SCALE * (degree * (degree + 1)).astype(F32) / float(NW * NW)
-    damp = 1.0 / (1.0 + DIFFUSION * lam * lam)
-    coupling = DT * DT * lam
-    diag = [1.0 + coupling * k[a][a] for a in range(2)]
-    cross = [coupling * k[0][1], coupling * k[1][0]]
-    inverse = 1.0 / (diag[0] * diag[1] - cross[0] * cross[1])
-    upper = row < 4
-    here = (row >> 2) == (group & 1)
-    for t in range(TRAJ):
+    gs = [[g[a][0] * s[0][b] + g[a][1] * s[1][b] for b in range(2)] for a in range(2)]
+    first_pair = lax.axis_index("space") * LOCAL + pl.program_id(0) * GROUP
+    fields = project_rows(back_ref)
+    row8, _ = row_col(8, WIDTH)
+    upper = row8 < 4
+    _, col = row_col(1, WIDTH)
+    for k in range(GROUP):
+        pair = first_pair + k
+        lhs = jnp.concatenate([rows[32 * k : 32 * k + 32] for rows in fields], axis=0)
+        sums = lax.dot_general(
+            lhs, leg_ref[k], (((1,), (1,)), ((), ())), preferred_element_type=F32
+        )
+        leading = col < NW - pair
+        offset = jnp.where(leading, col, col - (NW - pair))
+        parity = (1 - 2 * (offset & 1)).astype(F32)
+        degree = jnp.where(leading, pair, NW - 1 - pair) + offset
+        lam = WAVE_SCALE * (degree * (degree + 1)).astype(F32) / float(NW * NW)
+        damp = 1.0 / (1.0 + DIFFUSION * lam * lam)
+        coupling = DT * DT * lam
+        diag = [1.0 + coupling * gs[a][a] for a in range(2)]
+        cross = [coupling * gs[0][1], coupling * gs[1][0]]
+        inverse = 1.0 / (diag[0] * diag[1] - cross[0] * cross[1])
+        weight = [[DT * lam * g[a][b] for b in range(2)] for a in range(2)]
+        left = jnp.broadcast_to(leading, (8, WIDTH))
 
         def moved(f):
-            return state_ref[0, t, 8 * f : 8 * f + 8, 0:WIDTH] + DT * tend[t * FIELDS + f]
-
-        def place(f, value):
-            turned = pltpu.roll(value, 4, 0)
-            for part in range(2):
-                both = jnp.where(upper, turned, value) if part else jnp.where(upper, value, turned)
-                slot = new_ref.at[2 * (t * FIELDS + f) + part, group >> 1]
-                slot[...] = jnp.where(here, both, slot[...])
+            part = []
+            for r in range(2):
+                first = 32 * f + 16 * r
+                part.append(sums[first : first + 8] + parity * sums[first + 8 : first + 16])
+            near = jnp.where(upper, part[0], pltpu.roll(part[1], 4, 0))
+            far = jnp.where(upper, pltpu.roll(part[0], 4, 0), part[1])
+            old = jnp.concatenate([state_ref[0, 2 * f, k], state_ref[0, 2 * f + 1, k]], axis=0)
+            return old + DT * jnp.where(left, near, far)
+
+        def store(f, value):
+            out_ref[2 * f, k] = value[0:4]
+            out_ref[2 * f + 1, k] = value[4:8]
 
         for a in range(2):
-            place(a, damp * moved(a))
+            store(a, damp * moved(a))
         heat = [moved(4), moved(5)]
-        right = [
-            moved(2 + a) + DT * lam * (g[a][0] * heat[0] + g[a][1] * heat[1]) for a in range(2)
-        ]
+        right = [moved(2 + a) + (weight[a][0] * heat[0] + weight[a][1] * heat[1]) for a in range(2)]
         new = [
             (diag[1] * right[0] - cross[0] * right[1]) * inverse,
             (diag[0] * right[1] - cross[1] * right[0]) * inverse,
         ]
         for a in range(2):
-            place(2 + a, damp * new[a])
-            place(4 + a, damp * (heat[a] - DT * (s[a][0] * new[0] + s[a][1] * new[1])))
-
-
-def project_kernel(back_ref, leg_ref, state_ref, grav_ref, stab_ref, out_ref, new_ref):
-    group = pl.program_id(0)
-    first_pair = lax.axis_index("space") * LOCAL
-
-    def get(block, lane):
-        return back_ref[block, :, lane : lane + 128]
-
-    tend = project_group(group, first_pair, get, leg_ref)
-    semi_implicit(first_pair + group * GROUP, group, state_ref, tend, grav_ref, stab_ref, new_ref)
-
-    @pl.when(group == GROUPS - 1)
-    def _():
-        def finish(t, _):
-            for c in range(2 * FIELDS):
-                for tile in range(3):
-                    rows = min(8, LOCAL - 8 * tile)
-                    value = new_ref[2 * FIELDS * t + c, tile, 0:rows, :]
-                    out_ref[t, c, 8 * tile : 8 * tile + rows, :] = value
-            return 0
-
-        lax.fori_loop(0, TRAJ, finish, 0)
-
-
-def resident(shape):
-    return pl.BlockSpec(shape, lambda *_: (0,) * len(shape))
-
-
-STATE = (TRAJ, 2 * FIELDS, LOCAL, WIDTH)
+            store(2 + a, damp * new[a])
+            store(4 + a, damp * (heat[a] - DT * (s[a][0] * new[0] + s[a][1] * new[1])))
+
+
+STATE = (2 * FIELDS, LOCAL, TRAJ, WIDTH)
 LEG_BLOCK = pl.BlockSpec((GROUP, WIDTH, NHALF), lambda g: (g, 0, 0))
 BAND_BLOCK = pl.BlockSpec((SPACE, 16, LANES), lambda g: (0, g, 0))
 
@@ -572,11 +623,11 @@
     vmem = pl.BlockSpec(memory_space=pltpu.VMEM)
     smem = pl.BlockSpec(memory_space=pltpu.SMEM)
     dma = pltpu.SemaphoreType.DMA
-    pieces = (2, GROUPS, MEMBERS, 2 * FIELDS * GROUP, WIDE // 2)
+    pieces = (2, GROUPS, MEMBERS, MIX, WIDE // 2)
     band = (4 * PAIRS, LANES)
     return pl.pallas_call(
         main_kernel,
-        in_specs=[smem, vmem, anywhere, anywhere, anywhere, vmem],
+        in_specs=[smem, anywhere, anywhere, anywhere, anywhere, vmem],
         out_specs=[anywhere, anywhere],
         out_shape=[
             jax.ShapeDtypeStruct((SPACE, ROWS, LANES), BF16),
@@ -587,6 +638,8 @@
             pltpu.VMEM((4 * PAIRS, NLON), BF16),
             pltpu.VMEM((NLON, 4 * PAIRS), BF16),
             pltpu.VMEM(GROUPED, F32),
+            pltpu.VMEM((2, GROUPS, TRAJ * MIX, WIDE), BF16),
+            pltpu.VMEM((TRAJ * MIX, WIDE), F32),
             pltpu.VMEM(pieces, BF16),
             pltpu.VMEM(pieces, BF16),
             pltpu.VMEM(pieces, BF16),
@@ -594,6 +647,7 @@
             pltpu.VMEM(band, BF16),
             pltpu.VMEM(band, BF16),
             pltpu.VMEM(band, BF16),
+            dma((GROUPS,)),
             dma((GROUPS,)),
             dma((2,)),
             dma,
@@ -613,7 +667,7 @@
             vmem_limit_bytes=60 * 1024 * 1024, collective_id=0, has_side_effects=True
         ),
         name="bands",
-    )(clones, spectra, legendre, jnp.asarray(tall), jnp.asarray(wide), sin_lat.reshape(1, NHALF))
+    )(clones.T, spectra, legendre, jnp.asarray(tall), jnp.asarray(wide), sin_lat.reshape(1, NHALF))
 
 
 def to_spectral(back, legendre, state, gravity, stability):
@@ -624,21 +678,20 @@
         in_specs=[
             BAND_BLOCK,
             LEG_BLOCK,
-            pl.BlockSpec((1,) + GROUPED[1:], lambda g: (g, 0, 0, 0)),
+            pl.BlockSpec((1,) + GROUPED[1:], lambda g: (g, 0, 0, 0, 0)),
             smem,
             smem,
         ],
-        out_specs=resident(STATE),
+        out_specs=pl.BlockSpec((2 * FIELDS, GROUP, TRAJ, WIDTH), lambda g: (0, g, 0, 0)),
         out_shape=jax.ShapeDtypeStruct(STATE, F32),
-        scratch_shapes=[pltpu.VMEM((TRAJ * 2 * FIELDS, 3, 8, WIDTH), F32)],
         compiler_params=pltpu.CompilerParams(vmem_limit_bytes=56 * 1024 * 1024),
         name="project",
     )(back, legendre, state, gravity, stability)
 
 
 def shards(spectra, legendre, sin_lat, gravity, stability, clones):
-    back, state = to_bands(spectra, legendre, sin_lat, clones)
-    return to_spectral(back, legendre, state, gravity, stability)
+    back, state = to_bands(spectra.transpose(1, 2, 0, 3), legendre, sin_lat, clones)
+    return to_spectral(back, legendre, state, gravity, stability).transpose(2, 0, 1, 3)
 
 
 def solution(mesh):

time: 138 us -> 124 us (0.90)
  local copies, waits for them, and re-layouts: 12.3 us -> 1.24 us
  Pallas kernels: 124 us -> 122 us
    unnamed x2 -> x0, local copies, waits for them, and re-layouts: 5.53 us -> none
    pallas_call x1 -> x0, local copies, waits for them, and re-layouts: 5.5 us -> none  [to_spectral(): pl.pallas_call(project_kernel, grid=(GROUPS,), in_specs=[BAND_BLOCK, LEG_...]
    pallas_call x1, Pallas kernels: 12.3 us -> 10.4 us  [to_spectral(): pl.pallas_call(project_kernel, grid=(GROUPS,), in_specs=[BAND_BLOCK, LEG_...]
where the time goes in v3:
time: 124 us; the launch traced here: 123 us
  Pallas kernels  122 us (98%)
  local copies, waits for them, and re-layouts  1.24 us (1%)
    pallas_call x1, Pallas kernels, to_bands(): pl.pallas_call(main_kernel, in_specs=[smem, anywhere, anywhere, anywhere,...  111 us
    pallas_call x1, Pallas kernels, to_spectral(): pl.pallas_call(project_kernel, grid=(GROUPS,), in_specs=[BAND_BLOCK, LEG_...  10.4 us

profile of v3, /device:TPU:1, one launch (start us, length us, event | category | flops | bytes accessed | tf_op | source)
XLA Modules:
  0.0 122.9 jit_solution(5439638438798374781)
XLA Ops:
  0.0 1.2 %reshape.3.sin_ref = f32[1,384]{1,0:T(1,128)} reshape(f32[384]{0:T(512)} %param.10) | data formatting | bytes 3072 | tf_op jit(solution)/shard_map/reshape | solution.py:670
  1.2 111.3 %bands.1 = (bf16[16,80,1152]{2,1,0:T(8,128)(2,1)}, f32[5,12,4,4,641]{4,3,2,1,0:T(4,128)}) custom-call(s32[2,4]{1,0:T(2,128)} %bitcast.4, f32[12,20,4,641]{3,2,1,0:T(4,128)} %bitcast.3, bf16[20,641,384]{2,1,0:T(8,128)(2,1)} %leg_ref.1, bf16[1280,1280]{1,0:T(8,128)(2,1)} %constant.4.clone.tall_any, bf16[1280,1280]{1,0:T(8,128)(2,1)} %constant.5.clone.wide_any, ...), custom_call_target="tpu_custom_call" | custom-call | tf_op jit(solution)/shard_map/bands/pallas_call | solution.py:628
  112.5 10.4 %project.1 = f32[12,20,4,641]{3,2,1,0:T(4,128)} custom-call(bf16[16,80,1152]{2,1,0:T(8,128)(2,1)} %get-tuple-element.7.back_ref, bf16[20,641,384]{2,1,0:T(8,128)(2,1)} %leg_ref.1, f32[5,12,4,4,641]{4,3,2,1,0:T(4,128)} %get-tuple-element.8.state_ref, f32[2,2]{1,0:T(2,128)} %grav_ref.1, f32[2,2]{1,0:T(2,128)} %stab_ref.1), custom_call_target="tpu_custom_call" | custom-call | tf_op jit(solution)/shard_map/project/pallas_call | solution.py:675

commit v4 on v3

--- a/solution.py
+++ b/solution.py
@@ -21,7 +21,6 @@
 SPACE = 16
 GROUP = 4
 GROUPS = LOCAL // GROUP
-ROWS = 4 * LOCAL
 FULL = 128 * FIELDS
 LANES = FULL + 64 * FIELDS
 PART = ((0, FULL), (FULL, LANES))
@@ -30,6 +29,8 @@
 WIDE = 768
 GROUPED = (GROUPS, 2 * FIELDS, GROUP, TRAJ, WIDTH)
 MIX = 2 * FIELDS * GROUP
+TILE = 16 * SPACE
+EARLY = 2
 MESH = pl.DeviceIdType.MESH
 DT = 0.25
 WAVE_SCALE = 16.0
@@ -40,7 +41,7 @@
 
 @functools.cache
 def zonal_tables():
-    pair = np.arange(PAIRS)
+    pair = np.arange(PAIRS).reshape(SPACE, GROUPS, GROUP).transpose(1, 0, 2).reshape(-1)
     order = np.stack([pair, NW - 1 - pair], axis=1)
     phase = (order[:, :, None] * np.arange(NLON)) % NLON
     angle = phase * (2.0 * math.pi / NLON)
@@ -111,7 +112,7 @@
 
 def latitude_rows(sin_ref, place):
     low = lax.broadcasted_iota(jnp.int32, (1, 128), 1) < 64
-    zero, one, two = (sin_ref[:, 128 * i : 128 * i + 128] for i in range(3))
+    zero, one, two = (sin_ref[128 * i : 128 * i + 128].reshape(1, 128) for i in range(3))
     swapped = pltpu.roll(two, 64, 1)
     second = (place & 1) == 1
     sign = jnp.where((place & 3) >= 2, -1.0, 1.0).astype(F32)
@@ -131,7 +132,7 @@
 
 def grid_forward(part, sines, f_ref, wide_ref, forcing_ref):
     start, stop = PART[part]
-    tile = 256
+    tile = TILE
 
     def step(i, _):
         rows = pl.ds(pl.multiple_of(i * tile, tile), tile)
@@ -257,8 +258,6 @@
     ag_recv,
     out_send,
     out_recv,
-    half_send,
-    half_recv,
     back_send,
     back_recv,
 ):
@@ -362,125 +361,128 @@
             axis=0,
         )
 
-    def outward(g, peer, source):
-        lanes = pl.ds(0, FULL)
-        return pltpu.make_async_remote_copy(
-            src_ref=send_ref.at[peer, pl.ds(g * 16, 16), lanes],
-            dst_ref=fourier_ref.at[pl.ds(source * ROWS + g * 16, 16), lanes],
-            send_sem=out_send.at[g, peer],
-            recv_sem=out_recv.at[g, source],
-            device_id={"space": peer},
-            device_id_type=MESH,
-        )
-
-    def outward_half(peer, source):
-        lanes = pl.ds(FULL, LANES - FULL)
-        return pltpu.make_async_remote_copy(
-            src_ref=send_ref.at[peer, :, lanes],
-            dst_ref=fourier_ref.at[pl.ds(source * ROWS, ROWS), lanes],
-            send_sem=half_send.at[peer],
-            recv_sem=half_recv.at[source],
-            device_id={"space": peer},
-            device_id_type=MESH,
-        )
-
-    def homeward(part, peer, source):
+    def outward(part, g, peer, source):
         start, stop = PART[part]
         lanes = pl.ds(start, stop - start)
         return pltpu.make_async_remote_copy(
-            src_ref=give_ref.at[pl.ds(peer * ROWS, ROWS), lanes],
-            dst_ref=back_ref.at[source, :, lanes],
-            send_sem=back_send.at[part, peer],
-            recv_sem=back_recv.at[part, source],
+            src_ref=send_ref.at[g, peer, :, lanes],
+            dst_ref=fourier_ref.at[pl.ds(g * TILE + source * 16, 16), lanes],
+            send_sem=out_send.at[part, g, peer],
+            recv_sem=out_recv.at[part, g, source],
             device_id={"space": peer},
             device_id_type=MESH,
         )
+
+    def homeward(part, g, peer, source):
+        start, stop = PART[part]
+        lanes = pl.ds(start, stop - start)
+        return pltpu.make_async_remote_copy(
+            src_ref=give_ref.at[pl.ds(g * TILE + peer * 16, 16), lanes],
+            dst_ref=back_ref.at[g, source, :, lanes],
+            send_sem=back_send.at[part, g, peer],
+            recv_sem=back_recv.at[part, g, source],
+            device_id={"space": peer},
+            device_id_type=MESH,
+        )
+
+    def own_out(g):
+        rows = pl.ds(g * TILE + place * 16, 16)
+        return pltpu.make_async_copy(send_ref.at[g, place], fourier_ref.at[rows], own_sem.at[0, g])
+
+    def own_back(g):
+        rows = pl.ds(g * TILE + place * 16, 16)
+        return pltpu.make_async_copy(give_ref.at[rows], back_ref.at[g, place], own_sem.at[1, g])
+
+    def each_group(body):
+        def one(g, _):
+            body(g)
+            return 0
+
+        lax.fori_loop(0, GROUPS, one, 0)
+
+    def send_out(part, g):
+        spread("space", SPACE, lambda peer: outward(part, g, peer, place).start())
 
     x_copy(0).wait()
     regroup(0)
     pl.semaphore_wait(barrier, SPACE + MEMBERS - 2)
     offer(0, 0)
 
-    def rest(g, _):
-        x_copy(g).wait()
-        regroup(g)
-        offer(0, g)
-        return 0
-
-    lax.fori_loop(1, GROUPS, rest, 0)
+    x_copy(1).wait()
+    regroup(1)
+    settle(0, 0)
+    offer(0, 1)
     keep, put_rows = keep_and_put(clones_ref, member)
-    settle(0, 0)
 
     def legendre_step(g, _):
-        @pl.when(g + 1 < GROUPS)
+        @pl.when(g + 2 < GROUPS)
+        def _():
+            x_copy(g + 2).wait()
+            regroup(g + 2)
+
+        arrived(0, g)
+
+        @pl.when((g > 0) & (g + 1 < GROUPS))
         def _():
             settle(0, g + 1)
 
-        arrived(0, g)
+        @pl.when((g > 0) & (g + 2 < GROUPS))
+        def _():
+            offer(0, g + 2)
+
         now = jnp.dot(keep, half_ref[0, g], preferred_element_type=F32)
         now_ref[...] = now + jnp.dot(put_rows, received(0, g), preferred_element_type=F32)
         leg_copy(g).wait()
 
         def put(block, lane, value):
-            send_ref[block, pl.ds(pl.multiple_of(g * 16, 16), 16), lane : lane + 128] = value
+            send_ref[g, block, :, lane : lane + 128] = value
 
         legendre_group(
             place * LOCAL + g * GROUP, now_ref, leg_ref.at[pl.ds(g * GROUP, GROUP)], put
         )
-        spread("space", SPACE, lambda peer: outward(g, peer, place).start())
+        send_out(0, g)
+        own_out(g).start()
+
+        @pl.when(g < EARLY)
+        def _():
+            send_out(1, g)
+
+        @pl.when(g == 0)
+        def _():
+            settle(0, 1)
+            offer(0, 2)
+
         return 0
 
     lax.fori_loop(0, GROUPS, legendre_step, 0)
-    own_out = pltpu.make_async_copy(
-        send_ref.at[place], fourier_ref.at[pl.ds(place * ROWS, ROWS)], own_sem.at[0]
-    )
-    own_out.start()
-    spread("space", SPACE, lambda peer: outward_half(peer, place).start())
-
-    def each_group(body):
-        def one(g, _):
-            body(g)
-            return 0
-
-        lax.fori_loop(0, GROUPS, one, 0)
-
+
+    def send_late(g, _):
+        send_out(1, g)
+        return 0
+
+    lax.fori_loop(EARLY, GROUPS, send_late, 0)
     each_group(lambda g: offer(1, g))
     wide_copy.wait()
     tall_copy.wait()
-    own_out.wait()
-    each_group(
-        lambda g: spread("space", SPACE, lambda peer: outward(g, peer, peer).wait_recv())
-    )
-    quarter = 4 * ROWS
+    each_group(lambda g: own_out(g).wait())
+
     for part in range(2):
-        if part == 1:
-            spread("space", SPACE, lambda peer: outward_half(peer, peer).wait_recv())
+        each_group(
+            lambda g: spread(
+                "space", SPACE, lambda peer: outward(part, g, peer, peer).wait_recv()
+            )
+        )
         grid_forward(part, sines[part], fourier_ref, wide_ref, forcing_ref)
 
-        def backward(i, _, part=part):
-            block = lax.rem((place >> 2) + i, 4)
-            rows = pl.ds(pl.multiple_of(block * quarter, quarter), quarter)
+        def backward(g):
+            rows = pl.ds(pl.multiple_of(g * TILE, TILE), TILE)
             grid_backward(part, sines[part], rows, forcing_ref, tall_ref, give_ref)
-
-            def one(j, _):
-                peer = block * 4 + lax.rem((place & 3) + j, 4)
-
-                @pl.when(peer != place)
-                def _():
-                    homeward(part, peer, place).start()
-
-                return 0
-
-            lax.fori_loop(0, 4, one, 0)
-            return 0
-
-        lax.fori_loop(0, 4, backward, 0)
+            spread("space", SPACE, lambda peer: homeward(part, g, peer, place).start())
+
+        each_group(backward)
         if part == 0:
             each_group(lambda g: settle(1, g))
-    own_back = pltpu.make_async_copy(
-        give_ref.at[pl.ds(place * ROWS, ROWS)], back_ref.at[place], own_sem.at[1]
-    )
-    own_back.start()
+    each_group(lambda g: own_back(g).start())
 
     placing = place_rows(clones_ref, member)
     row, _ = row_col(TRAJ, WIDTH)
@@ -509,14 +511,23 @@
         each_group(
             lambda g: spread("member", MEMBERS, lambda peer: gather(q, g, peer, member).wait_send())
         )
-    each_group(
-        lambda g: spread("space", SPACE, lambda peer: outward(g, peer, place).wait_send())
-    )
-    spread("space", SPACE, lambda peer: outward_half(peer, place).wait_send())
     for part in range(2):
-        spread("space", SPACE, lambda peer: homeward(part, peer, place).wait_send())
-        spread("space", SPACE, lambda peer: homeward(part, peer, peer).wait_recv())
-    own_back.wait()
+        each_group(
+            lambda g: spread(
+                "space", SPACE, lambda peer: outward(part, g, peer, place).wait_send()
+            )
+        )
+        each_group(
+            lambda g: spread(
+                "space", SPACE, lambda peer: homeward(part, g, peer, place).wait_send()
+            )
+        )
+        each_group(
+            lambda g: spread(
+                "space", SPACE, lambda peer: homeward(part, g, peer, peer).wait_recv()
+            )
+        )
+    each_group(lambda g: own_back(g).wait())
     state_copy.wait()
 
 
@@ -533,7 +544,7 @@
     def column(odd, lane):
         return jnp.concatenate(
             [
-                back_ref[4 * t + 2 * side + odd, :, lane : lane + 128]
+                back_ref[0, 4 * t + 2 * side + odd, :, lane : lane + 128]
                 for t in range(TRAJ)
                 for side in range(2)
             ],
@@ -614,7 +625,7 @@
 
 STATE = (2 * FIELDS, LOCAL, TRAJ, WIDTH)
 LEG_BLOCK = pl.BlockSpec((GROUP, WIDTH, NHALF), lambda g: (g, 0, 0))
-BAND_BLOCK = pl.BlockSpec((SPACE, 16, LANES), lambda g: (0, g, 0))
+BAND_BLOCK = pl.BlockSpec((1, SPACE, 16, LANES), lambda g: (g, 0, 0, 0))
 
 
 def to_bands(spectra, legendre, sin_lat, clones):
@@ -630,7 +641,7 @@
         in_specs=[smem, anywhere, anywhere, anywhere, anywhere, vmem],
         out_specs=[anywhere, anywhere],
         out_shape=[
-            jax.ShapeDtypeStruct((SPACE, ROWS, LANES), BF16),
+            jax.ShapeDtypeStruct((GROUPS, SPACE, 16, LANES), BF16),
             jax.ShapeDtypeStruct(GROUPED, F32),
         ],
         scratch_shapes=[
@@ -643,7 +654,7 @@
             pltpu.VMEM(pieces, BF16),
             pltpu.VMEM(pieces, BF16),
             pltpu.VMEM(pieces, BF16),
-            pltpu.VMEM((SPACE, ROWS, LANES), BF16),
+            pltpu.VMEM((GROUPS, SPACE, 16, LANES), BF16),
             pltpu.VMEM(band, BF16),
             pltpu.VMEM(band, BF16),
             pltpu.VMEM(band, BF16),
@@ -651,23 +662,21 @@
             dma((GROUPS,)),
             dma((2,)),
             dma,
-            dma((2,)),
+            dma((2, GROUPS)),
             dma((2, GROUPS, MEMBERS)),
             dma((2, GROUPS, MEMBERS)),
             dma((2, GROUPS, MEMBERS)),
             dma((2, GROUPS, MEMBERS)),
-            dma((GROUPS, SPACE)),
-            dma((GROUPS, SPACE)),
-            dma((SPACE,)),
-            dma((SPACE,)),
-            dma((2, SPACE)),
-            dma((2, SPACE)),
+            dma((2, GROUPS, SPACE)),
+            dma((2, GROUPS, SPACE)),
+            dma((2, GROUPS, SPACE)),
+            dma((2, GROUPS, SPACE)),
         ],
         compiler_params=pltpu.CompilerParams(
             vmem_limit_bytes=60 * 1024 * 1024, collective_id=0, has_side_effects=True
         ),
         name="bands",
-    )(clones.T, spectra, legendre, jnp.asarray(tall), jnp.asarray(wide), sin_lat.reshape(1, NHALF))
+    )(clones.T, spectra, legendre, jnp.asarray(tall), jnp.asarray(wide), sin_lat)
 
 
 def to_spectral(back, legendre, state, gravity, stability):

time: 124 us -> 123 us (level)
  local copies, waits for them, and re-layouts: 1.24 us -> 0 us
    pallas_call x1, Pallas kernels: 111 us -> 113 us  [to_bands(): pl.pallas_call(main_kernel, in_specs=[smem, anywhere, anywhere, anywhere,...]
    reshape x1 -> x0, local copies, waits for them, and re-layouts: 1.24 us -> none  [to_bands(): sin_lat.reshape(1, NHALF)]
where the time goes in v4:
time: 123 us
  Pallas kernels  123 us (100%)
    pallas_call x1, Pallas kernels, to_bands(): pl.pallas_call(main_kernel, in_specs=[smem, anywhere, anywhere, anywhere,...  113 us
    pallas_call x1, Pallas kernels, to_spectral(): pl.pallas_call(project_kernel, grid=(GROUPS,), in_specs=[BAND_BLOCK, LEG_...  10.4 us

profile of v4, /device:TPU:1, one launch (start us, length us, event | category | flops | bytes accessed | tf_op | source)
XLA Modules:
  0.0 123.1 jit_solution(16084673257167817351)
XLA Ops:
  0.0 112.7 %bands.1 = (bf16[5,16,16,1152]{3,2,1,0:T(8,128)(2,1)}, f32[5,12,4,4,641]{4,3,2,1,0:T(4,128)}) custom-call(s32[2,4]{1,0:T(2,128)} %bitcast.4, f32[12,20,4,641]{3,2,1,0:T(4,128)} %bitcast.3, bf16[20,641,384]{2,1,0:T(8,128)(2,1)} %leg_ref.1, bf16[1280,1280]{1,0:T(8,128)(2,1)} %constant.4.clone.tall_any, bf16[1280,1280]{1,0:T(8,128)(2,1)} %constant.5.clone.wide_any, ...), custom_call_target="tpu_custom_call" | custom-call | tf_op jit(solution)/shard_map/bands/pallas_call | solution.py:639
  112.7 10.4 %project.1 = f32[12,20,4,641]{3,2,1,0:T(4,128)} custom-call(bf16[5,16,16,1152]{3,2,1,0:T(8,128)(2,1)} %get-tuple-element.7.back_ref, bf16[20,641,384]{2,1,0:T(8,128)(2,1)} %leg_ref.1, f32[5,12,4,4,641]{4,3,2,1,0:T(4,128)} %get-tuple-element.8.state_ref, f32[2,2]{1,0:T(2,128)} %grav_ref.1, f32[2,2]{1,0:T(2,128)} %stab_ref.1), custom_call_target="tpu_custom_call" | custom-call | tf_op jit(solution)/shard_map/project/pallas_call | solution.py:684

commit v5 on v4

--- a/solution.py
+++ b/solution.py
@@ -25,6 +25,7 @@
 LANES = FULL + 64 * FIELDS
 PART = ((0, FULL), (FULL, LANES))
 MEMBERS = 8
+CHIPS = 4
 KILLED = 4
 WIDE = 768
 GROUPED = (GROUPS, 2 * FIELDS, GROUP, TRAJ, WIDTH)
@@ -241,6 +242,8 @@
     half_ref,
     now_ref,
     hand_ref,
+    core_ref,
+    pair_ref,
     landed_ref,
     shared_ref,
     send_ref,
@@ -252,6 +255,8 @@
     table_sem,
     state_sem,
     own_sem,
+    core_send,
+    core_recv,
     rs_send,
     rs_recv,
     ag_send,
@@ -263,6 +268,9 @@
 ):
     member = lax.axis_index("member")
     place = lax.axis_index("space")
+    core = member & 1
+    chip = member >> 1
+    partner = member + 1 - 2 * core
     sines = latitude_rows(sin_ref, place)
 
     def x_copy(g):
@@ -297,26 +305,43 @@
         ),
     )
 
+    def across(q, g):
+        return pltpu.make_async_remote_copy(
+            src_ref=hand_ref.at[q, g, 1 - core],
+            dst_ref=core_ref.at[q, g],
+            send_sem=core_send.at[q, g],
+            recv_sem=core_recv.at[q, g],
+            device_id={"member": partner},
+            device_id_type=MESH,
+        )
+
     def scatter(q, g, peer, source):
         return pltpu.make_async_remote_copy(
-            src_ref=hand_ref.at[q, g, peer],
+            src_ref=pair_ref.at[q, g, peer],
             dst_ref=landed_ref.at[q, g, source],
             send_sem=rs_send.at[q, g, peer],
             recv_sem=rs_recv.at[q, g, source],
-            device_id={"member": peer},
+            device_id={"member": 2 * peer + core},
             device_id_type=MESH,
         )
 
     def gather(q, g, peer, source):
         return pltpu.make_async_remote_copy(
-            src_ref=shared_ref.at[q, g, source],
-            dst_ref=shared_ref.at[q, g, source],
+            src_ref=shared_ref.at[q, g, source & 1, source >> 1],
+            dst_ref=shared_ref.at[q, g, source & 1, source >> 1],
             send_sem=ag_send.at[q, g, peer],
             recv_sem=ag_recv.at[q, g, source],
             device_id={"member": peer},
             device_id_type=MESH,
         )
 
+    def other_chips(body):
+        def one(d, _):
+            body(lax.rem(chip + d, CHIPS))
+            return 0
+
+        lax.fori_loop(1, CHIPS, one, 0)
+
     def regroup(g):
         rows = jnp.concatenate(
             [xg_ref[g, c, p] for c in range(2 * FIELDS) for p in range(GROUP)], axis=0
@@ -335,18 +360,22 @@
         value = jnp.dot(selection, half_ref[q, g], preferred_element_type=F32).astype(BF16)
         for entry in range(KILLED):
             rows = slice(MIX * entry, MIX * entry + MIX)
-            hand_ref[q, g, 2 * entry] = value[rows, 0 : WIDE // 2]
-            hand_ref[q, g, 2 * entry + 1] = value[rows, WIDE // 2 : WIDE]
-        spread("member", MEMBERS, lambda peer: scatter(q, g, peer, member).start())
+            hand_ref[q, g, 0, entry] = value[rows, 0 : WIDE // 2]
+            hand_ref[q, g, 1, entry] = value[rows, WIDE // 2 : WIDE]
+        across(q, g).start()
+
+    def combine(q, g):
+        across(q, g).wait_recv()
+        total = hand_ref[q, g, core].astype(F32) + core_ref[q, g].astype(F32)
+        pair_ref[q, g] = total.astype(BF16)
+        other_chips(lambda peer: scatter(q, g, peer, chip).start())
 
     def settle(q, g):
-        spread("member", MEMBERS, lambda peer: scatter(q, g, peer, peer).wait_recv())
-
-        def add(d, total):
-            return total + landed_ref[q, g, lax.rem(member + d, MEMBERS)].astype(F32)
-
-        total = lax.fori_loop(1, MEMBERS, add, hand_ref[q, g, member].astype(F32))
-        shared_ref[q, g, member] = total.astype(BF16)
+        other_chips(lambda peer: scatter(q, g, peer, peer).wait_recv())
+        total = pair_ref[q, g, chip].astype(F32)
+        for d in range(1, CHIPS):
+            total = total + landed_ref[q, g, lax.rem(chip + d, CHIPS)].astype(F32)
+        shared_ref[q, g, core, chip] = total.astype(BF16)
         spread("member", MEMBERS, lambda peer: gather(q, g, peer, member).start())
 
     def arrived(q, g):
@@ -355,7 +384,7 @@
     def received(q, g):
         return jnp.concatenate(
             [
-                jnp.concatenate([shared_ref[q, g, 2 * e], shared_ref[q, g, 2 * e + 1]], axis=1)
+                jnp.concatenate([shared_ref[q, g, 0, e], shared_ref[q, g, 1, e]], axis=1)
                 for e in range(KILLED)
             ],
             axis=0,
@@ -410,26 +439,31 @@
 
     x_copy(1).wait()
     regroup(1)
+    offer(0, 1)
+    combine(0, 0)
+    x_copy(2).wait()
+    regroup(2)
+    offer(0, 2)
+    combine(0, 1)
+    keep, put_rows = keep_and_put(clones_ref, member)
     settle(0, 0)
-    offer(0, 1)
-    keep, put_rows = keep_and_put(clones_ref, member)
 
     def legendre_step(g, _):
+        @pl.when(g + 3 < GROUPS)
+        def _():
+            x_copy(g + 3).wait()
+            regroup(g + 3)
+            offer(0, g + 3)
+
         @pl.when(g + 2 < GROUPS)
         def _():
-            x_copy(g + 2).wait()
-            regroup(g + 2)
-
-        arrived(0, g)
-
-        @pl.when((g > 0) & (g + 1 < GROUPS))
+            combine(0, g + 2)
+
+        @pl.when(g + 1 < GROUPS)
         def _():
             settle(0, g + 1)
 
-        @pl.when((g > 0) & (g + 2 < GROUPS))
-        def _():
-            offer(0, g + 2)
-
+        arrived(0, g)
         now = jnp.dot(keep, half_ref[0, g], preferred_element_type=F32)
         now_ref[...] = now + jnp.dot(put_rows, received(0, g), preferred_element_type=F32)
         leg_copy(g).wait()
@@ -447,11 +481,6 @@
         def _():
             send_out(1, g)
 
-        @pl.when(g == 0)
-        def _():
-            settle(0, 1)
-            offer(0, 2)
-
         return 0
 
     lax.fori_loop(0, GROUPS, legendre_step, 0)
@@ -462,6 +491,7 @@
 
     lax.fori_loop(EARLY, GROUPS, send_late, 0)
     each_group(lambda g: offer(1, g))
+    each_group(lambda g: combine(1, g))
     wide_copy.wait()
     tall_copy.wait()
     each_group(lambda g: own_out(g).wait())
@@ -505,9 +535,8 @@
     state_copy = pltpu.make_async_copy(xg_ref, state_ref, state_sem)
     state_copy.start()
     for q in range(2):
-        each_group(
-            lambda g: spread("member", MEMBERS, lambda peer: scatter(q, g, peer, peer).wait_send())
-        )
+        each_group(lambda g: across(q, g).wait_send())
+        each_group(lambda g: other_chips(lambda peer: scatter(q, g, peer, chip).wait_send()))
         each_group(
             lambda g: spread("member", MEMBERS, lambda peer: gather(q, g, peer, member).wait_send())
         )
@@ -634,7 +663,7 @@
     vmem = pl.BlockSpec(memory_space=pltpu.VMEM)
     smem = pl.BlockSpec(memory_space=pltpu.SMEM)
     dma = pltpu.SemaphoreType.DMA
-    pieces = (2, GROUPS, MEMBERS, MIX, WIDE // 2)
+    pieces = (KILLED, MIX, WIDE // 2)
     band = (4 * PAIRS, LANES)
     return pl.pallas_call(
         main_kernel,
@@ -651,9 +680,11 @@
             pltpu.VMEM(GROUPED, F32),
             pltpu.VMEM((2, GROUPS, TRAJ * MIX, WIDE), BF16),
             pltpu.VMEM((TRAJ * MIX, WIDE), F32),
-            pltpu.VMEM(pieces, BF16),
-            pltpu.VMEM(pieces, BF16),
-            pltpu.VMEM(pieces, BF16),
+            pltpu.VMEM((2, GROUPS, 2) + pieces, BF16),
+            pltpu.VMEM((2, GROUPS) + pieces, BF16),
+            pltpu.VMEM((2, GROUPS) + pieces, BF16),
+            pltpu.VMEM((2, GROUPS) + pieces, BF16),
+            pltpu.VMEM((2, GROUPS, 2) + pieces, BF16),
             pltpu.VMEM((GROUPS, SPACE, 16, LANES), BF16),
             pltpu.VMEM(band, BF16),
             pltpu.VMEM(band, BF16),
@@ -663,8 +694,10 @@
             dma((2,)),
             dma,
             dma((2, GROUPS)),
-            dma((2, GROUPS, MEMBERS)),
-            dma((2, GROUPS, MEMBERS)),
+            dma((2, GROUPS)),
+            dma((2, GROUPS)),
+            dma((2, GROUPS, CHIPS)),
+            dma((2, GROUPS, CHIPS)),
             dma((2, GROUPS, MEMBERS)),
             dma((2, GROUPS, MEMBERS)),
             dma((2, GROUPS, SPACE)),

time: 123 us -> 109 us (0.89)
  Pallas kernels: 123 us -> 109 us
    pallas_call x1, Pallas kernels: 113 us -> 98.9 us  [to_bands(): pl.pallas_call(main_kernel, in_specs=[smem, anywhere, anywhere, anywhere,...]
where the time goes in v5:
time: 109 us
  Pallas kernels  109 us (100%)
    pallas_call x1, Pallas kernels, to_bands(): pl.pallas_call(main_kernel, in_specs=[smem, anywhere, anywhere, anywhere,...  98.9 us
    pallas_call x1, Pallas kernels, to_spectral(): pl.pallas_call(project_kernel, grid=(GROUPS,), in_specs=[BAND_BLOCK, LEG_...  10.4 us

profile of v5, /device:TPU:1, one launch (start us, length us, event | category | flops | bytes accessed | tf_op | source)
XLA Modules:
  0.0 109.3 jit_solution(8753631672311906555)
XLA Ops:
  0.0 98.9 %bands.1 = (bf16[5,16,16,1152]{3,2,1,0:T(8,128)(2,1)}, f32[5,12,4,4,641]{4,3,2,1,0:T(4,128)}) custom-call(s32[2,4]{1,0:T(2,128)} %bitcast.4, f32[12,20,4,641]{3,2,1,0:T(4,128)} %bitcast.3, bf16[20,641,384]{2,1,0:T(8,128)(2,1)} %leg_ref.1, bf16[1280,1280]{1,0:T(8,128)(2,1)} %constant.4.clone.tall_any, bf16[1280,1280]{1,0:T(8,128)(2,1)} %constant.5.clone.wide_any, ...), custom_call_target="tpu_custom_call" | custom-call | tf_op jit(solution)/shard_map/bands/pallas_call | solution.py:668
  98.9 10.4 %project.1 = f32[12,20,4,641]{3,2,1,0:T(4,128)} custom-call(bf16[5,16,16,1152]{3,2,1,0:T(8,128)(2,1)} %get-tuple-element.7.back_ref, bf16[20,641,384]{2,1,0:T(8,128)(2,1)} %leg_ref.1, f32[5,12,4,4,641]{4,3,2,1,0:T(4,128)} %get-tuple-element.8.state_ref, f32[2,2]{1,0:T(2,128)} %grav_ref.1, f32[2,2]{1,0:T(2,128)} %stab_ref.1), custom_call_target="tpu_custom_call" | custom-call | tf_op jit(solution)/shard_map/project/pallas_call | solution.py:717

commit v6 on v5

--- a/solution.py
+++ b/solution.py
@@ -216,6 +216,97 @@
     return one_hot((entry == by_trajectory(found, row & 3)) & ((row >> 2) == col - MIX * entry))
 
 
+def unmix():
+    row, col = row_col(128, 128)
+    t, half, side, part, pair = row & 3, (row >> 2) & 1, (row >> 3) & 1, (row >> 4) & 1, row >> 5
+    return one_hot(col == 32 * t + 16 * side + 4 * pair + 2 * half + part)
+
+
+def project_rows(back_ref):
+    low = lax.broadcasted_iota(jnp.int32, (128, 128), 1) < 64
+    order = unmix()
+
+    def column(odd, lane):
+        return jnp.concatenate(
+            [
+                back_ref[4 * t + 2 * side + odd, :, lane : lane + 128]
+                for t in range(TRAJ)
+                for side in range(2)
+            ],
+            axis=0,
+        )
+
+    fields = []
+    for level in range(FIELDS // 2):
+        lanes = [256 * level, 256 * level + 128, FULL + 128 * level]
+        mixed = jnp.concatenate([column(odd, lane) for lane in lanes for odd in range(2)], axis=1)
+        rows = jnp.dot(order, mixed, preferred_element_type=F32)
+        a, b = rows[:, 512:640], rows[:, 640:768]
+        last = (
+            jnp.where(low, a, pltpu.roll(b, 64, 1)),
+            jnp.where(low, pltpu.roll(a, 64, 1), b),
+        )
+        for h in range(2):
+            fields.append(
+                jnp.concatenate([rows[:, 256 * h : 256 * h + 256], last[h]], axis=1).astype(BF16)
+            )
+    return fields
+
+
+def project_group(first_pair, back_ref, leg_ref, state_ref, grav_ref, stab_ref):
+    g = [[grav_ref[a, b] for b in range(2)] for a in range(2)]
+    s = [[stab_ref[a, b] for b in range(2)] for a in range(2)]
+    gs = [[g[a][0] * s[0][b] + g[a][1] * s[1][b] for b in range(2)] for a in range(2)]
+    fields = project_rows(back_ref)
+    row8, _ = row_col(8, WIDTH)
+    upper = row8 < 4
+    _, col = row_col(1, WIDTH)
+    for k in range(GROUP):
+        pair = first_pair + k
+        lhs = jnp.concatenate([rows[32 * k : 32 * k + 32] for rows in fields], axis=0)
+        sums = lax.dot_general(
+            lhs, leg_ref[k], (((1,), (1,)), ((), ())), preferred_element_type=F32
+        )
+        leading = col < NW - pair
+        offset = jnp.where(leading, col, col - (NW - pair))
+        parity = (1 - 2 * (offset & 1)).astype(F32)
+        degree = jnp.where(leading, pair, NW - 1 - pair) + offset
+        lam = WAVE_SCALE * (degree * (degree + 1)).astype(F32) / float(NW * NW)
+        damp = 1.0 / (1.0 + DIFFUSION * lam * lam)
+        coupling = DT * DT * lam
+        diag = [1.0 + coupling * gs[a][a] for a in range(2)]
+        cross = [coupling * gs[0][1], coupling * gs[1][0]]
+        inverse = 1.0 / (diag[0] * diag[1] - cross[0] * cross[1])
+        weight = [[DT * lam * g[a][b] for b in range(2)] for a in range(2)]
+        left = jnp.broadcast_to(leading, (8, WIDTH))
+
+        def moved(f):
+            part = []
+            for r in range(2):
+                first = 32 * f + 16 * r
+                part.append(sums[first : first + 8] + parity * sums[first + 8 : first + 16])
+            near = jnp.where(upper, part[0], pltpu.roll(part[1], 4, 0))
+            far = jnp.where(upper, pltpu.roll(part[0], 4, 0), part[1])
+            old = jnp.concatenate([state_ref[2 * f, k], state_ref[2 * f + 1, k]], axis=0)
+            return old + DT * jnp.where(left, near, far)
+
+        def store(f, value):
+            state_ref[2 * f, k] = value[0:4]
+            state_ref[2 * f + 1, k] = value[4:8]
+
+        for a in range(2):
+            store(a, damp * moved(a))
+        heat = [moved(4), moved(5)]
+        right = [moved(2 + a) + (weight[a][0] * heat[0] + weight[a][1] * heat[1]) for a in range(2)]
+        new = [
+            (diag[1] * right[0] - cross[0] * right[1]) * inverse,
+            (diag[0] * right[1] - cross[1] * right[0]) * inverse,
+        ]
+        for a in range(2):
+            store(2 + a, damp * new[a])
+            store(4 + a, damp * (heat[a] - DT * (s[a][0] * new[0] + s[a][1] * new[1])))
+
+
 def spread(axis, count, body):
     me = lax.axis_index(axis)
 
@@ -233,8 +324,9 @@
     tall_any,
     wide_any,
     sin_ref,
-    back_ref,
-    state_ref,
+    grav_ref,
+    stab_ref,
+    new_any,
     leg_ref,
     tall_ref,
     wide_ref,
@@ -250,6 +342,7 @@
     fourier_ref,
     forcing_ref,
     give_ref,
+    back_ref,
     x_sem,
     leg_sem,
     table_sem,
@@ -531,9 +624,28 @@
                 new = value[first : first + TRAJ, 0:WIDTH]
                 xg_ref[g, c, p] = jnp.where(killed < KILLED, new, xg_ref[g, c, p])
 
-    each_group(complete)
-    state_copy = pltpu.make_async_copy(xg_ref, state_ref, state_sem)
-    state_copy.start()
+    def new_copy(g):
+        some = pl.ds(g * GROUP, GROUP)
+        return pltpu.make_async_copy(xg_ref.at[g], new_any.at[:, some], state_sem.at[g])
+
+    def project(g):
+        complete(g)
+        own_back(g).wait()
+        for part in range(2):
+            spread(
+                "space", SPACE, lambda peer: homeward(part, g, peer, peer).wait_recv()
+            )
+        project_group(
+            place * LOCAL + g * GROUP,
+            back_ref.at[g],
+            leg_ref.at[pl.ds(g * GROUP, GROUP)],
+            xg_ref.at[g],
+            grav_ref,
+            stab_ref,
+        )
+        new_copy(g).start()
+
+    each_group(project)
     for q in range(2):
         each_group(lambda g: across(q, g).wait_send())
         each_group(lambda g: other_chips(lambda peer: scatter(q, g, peer, chip).wait_send()))
@@ -551,113 +663,13 @@
                 "space", SPACE, lambda peer: homeward(part, g, peer, place).wait_send()
             )
         )
-        each_group(
-            lambda g: spread(
-                "space", SPACE, lambda peer: homeward(part, g, peer, peer).wait_recv()
-            )
-        )
-    each_group(lambda g: own_back(g).wait())
-    state_copy.wait()
-
-
-def unmix():
-    row, col = row_col(128, 128)
-    t, half, side, part, pair = row & 3, (row >> 2) & 1, (row >> 3) & 1, (row >> 4) & 1, row >> 5
-    return one_hot(col == 32 * t + 16 * side + 4 * pair + 2 * half + part)
-
-
-def project_rows(back_ref):
-    low = lax.broadcasted_iota(jnp.int32, (128, 128), 1) < 64
-    order = unmix()
-
-    def column(odd, lane):
-        return jnp.concatenate(
-            [
-                back_ref[0, 4 * t + 2 * side + odd, :, lane : lane + 128]
-                for t in range(TRAJ)
-                for side in range(2)
-            ],
-            axis=0,
-        )
-
-    fields = []
-    for level in range(FIELDS // 2):
-        lanes = [256 * level, 256 * level + 128, FULL + 128 * level]
-        mixed = jnp.concatenate([column(odd, lane) for lane in lanes for odd in range(2)], axis=1)
-        rows = jnp.dot(order, mixed, preferred_element_type=F32)
-        a, b = rows[:, 512:640], rows[:, 640:768]
-        last = (
-            jnp.where(low, a, pltpu.roll(b, 64, 1)),
-            jnp.where(low, pltpu.roll(a, 64, 1), b),
-        )
-        for h in range(2):
-            fields.append(
-                jnp.concatenate([rows[:, 256 * h : 256 * h + 256], last[h]], axis=1).astype(BF16)
-            )
-    return fields
-
-
-def project_kernel(back_ref, leg_ref, state_ref, grav_ref, stab_ref, out_ref):
-    g = [[grav_ref[a, b] for b in range(2)] for a in range(2)]
-    s = [[stab_ref[a, b] for b in range(2)] for a in range(2)]
-    gs = [[g[a][0] * s[0][b] + g[a][1] * s[1][b] for b in range(2)] for a in range(2)]
-    first_pair = lax.axis_index("space") * LOCAL + pl.program_id(0) * GROUP
-    fields = project_rows(back_ref)
-    row8, _ = row_col(8, WIDTH)
-    upper = row8 < 4
-    _, col = row_col(1, WIDTH)
-    for k in range(GROUP):
-        pair = first_pair + k
-        lhs = jnp.concatenate([rows[32 * k : 32 * k + 32] for rows in fields], axis=0)
-        sums = lax.dot_general(
-            lhs, leg_ref[k], (((1,), (1,)), ((), ())), preferred_element_type=F32
-        )
-        leading = col < NW - pair
-        offset = jnp.where(leading, col, col - (NW - pair))
-        parity = (1 - 2 * (offset & 1)).astype(F32)
-        degree = jnp.where(leading, pair, NW - 1 - pair) + offset
-        lam = WAVE_SCALE * (degree * (degree + 1)).astype(F32) / float(NW * NW)
-        damp = 1.0 / (1.0 + DIFFUSION * lam * lam)
-        coupling = DT * DT * lam
-        diag = [1.0 + coupling * gs[a][a] for a in range(2)]
-        cross = [coupling * gs[0][1], coupling * gs[1][0]]
-        inverse = 1.0 / (diag[0] * diag[1] - cross[0] * cross[1])
-        weight = [[DT * lam * g[a][b] for b in range(2)] for a in range(2)]
-        left = jnp.broadcast_to(leading, (8, WIDTH))
-
-        def moved(f):
-            part = []
-            for r in range(2):
-                first = 32 * f + 16 * r
-                part.append(sums[first : first + 8] + parity * sums[first + 8 : first + 16])
-            near = jnp.where(upper, part[0], pltpu.roll(part[1], 4, 0))
-            far = jnp.where(upper, pltpu.roll(part[0], 4, 0), part[1])
-            old = jnp.concatenate([state_ref[0, 2 * f, k], state_ref[0, 2 * f + 1, k]], axis=0)
-            return old + DT * jnp.where(left, near, far)
-
-        def store(f, value):
-            out_ref[2 * f, k] = value[0:4]
-            out_ref[2 * f + 1, k] = value[4:8]
-
-        for a in range(2):
-            store(a, damp * moved(a))
-        heat = [moved(4), moved(5)]
-        right = [moved(2 + a) + (weight[a][0] * heat[0] + weight[a][1] * heat[1]) for a in range(2)]
-        new = [
-            (diag[1] * right[0] - cross[0] * right[1]) * inverse,
-            (diag[0] * right[1] - cross[1] * right[0]) * inverse,
-        ]
-        for a in range(2):
-            store(2 + a, damp * new[a])
-            store(4 + a, damp * (heat[a] - DT * (s[a][0] * new[0] + s[a][1] * new[1])))
+    each_group(lambda g: new_copy(g).wait())
 
 
 STATE = (2 * FIELDS, LOCAL, TRAJ, WIDTH)
-LEG_BLOCK = pl.BlockSpec((GROUP, WIDTH, NHALF), lambda g: (g, 0, 0))
-BAND_BLOCK = pl.BlockSpec((1, SPACE, 16, LANES), lambda g: (g, 0, 0, 0))
-
-
-def to_bands(spectra, legendre, sin_lat, clones):
+
+
+def step(state, legendre, sin_lat, gravity, stability, clones):
     tall, wide = zonal_tables()
     anywhere = pl.BlockSpec(memory_space=pl.ANY)
     vmem = pl.BlockSpec(memory_space=pltpu.VMEM)
@@ -667,12 +679,9 @@
     band = (4 * PAIRS, LANES)
     return pl.pallas_call(
         main_kernel,
-        in_specs=[smem, anywhere, anywhere, anywhere, anywhere, vmem],
-        out_specs=[anywhere, anywhere],
-        out_shape=[
-            jax.ShapeDtypeStruct((GROUPS, SPACE, 16, LANES), BF16),
-            jax.ShapeDtypeStruct(GROUPED, F32),
-        ],
+        in_specs=[smem, anywhere, anywhere, anywhere, anywhere, vmem, smem, smem],
+        out_specs=anywhere,
+        out_shape=jax.ShapeDtypeStruct(STATE, F32),
         scratch_shapes=[
             pltpu.VMEM((LOCAL, WIDTH, NHALF), BF16),
             pltpu.VMEM((4 * PAIRS, NLON), BF16),
@@ -689,10 +698,11 @@
             pltpu.VMEM(band, BF16),
             pltpu.VMEM(band, BF16),
             pltpu.VMEM(band, BF16),
+            pltpu.VMEM((GROUPS, SPACE, 16, LANES), BF16),
             dma((GROUPS,)),
             dma((GROUPS,)),
             dma((2,)),
-            dma,
+            dma((GROUPS,)),
             dma((2, GROUPS)),
             dma((2, GROUPS)),
             dma((2, GROUPS)),
@@ -708,32 +718,22 @@
         compiler_params=pltpu.CompilerParams(
             vmem_limit_bytes=60 * 1024 * 1024, collective_id=0, has_side_effects=True
         ),
-        name="bands",
-    )(clones.T, spectra, legendre, jnp.asarray(tall), jnp.asarray(wide), sin_lat)
-
-
-def to_spectral(back, legendre, state, gravity, stability):
-    smem = pl.BlockSpec(memory_space=pltpu.SMEM)
-    return pl.pallas_call(
-        project_kernel,
-        grid=(GROUPS,),
-        in_specs=[
-            BAND_BLOCK,
-            LEG_BLOCK,
-            pl.BlockSpec((1,) + GROUPED[1:], lambda g: (g, 0, 0, 0, 0)),
-            smem,
-            smem,
-        ],
-        out_specs=pl.BlockSpec((2 * FIELDS, GROUP, TRAJ, WIDTH), lambda g: (0, g, 0, 0)),
-        out_shape=jax.ShapeDtypeStruct(STATE, F32),
-        compiler_params=pltpu.CompilerParams(vmem_limit_bytes=56 * 1024 * 1024),
-        name="project",
-    )(back, legendre, state, gravity, stability)
+        name="step",
+    )(
+        clones.T,
+        state,
+        legendre,
+        jnp.asarray(tall),
+        jnp.asarray(wide),
+        sin_lat,
+        gravity,
+        stability,
+    )
 
 
 def shards(spectra, legendre, sin_lat, gravity, stability, clones):
-    back, state = to_bands(spectra.transpose(1, 2, 0, 3), legendre, sin_lat, clones)
-    return to_spectral(back, legendre, state, gravity, stability).transpose(2, 0, 1, 3)
+    state = spectra.transpose(1, 2, 0, 3)
+    return step(state, legendre, sin_lat, gravity, stability, clones).transpose(2, 0, 1, 3)
 
 
 def solution(mesh):

time: 109 us -> 109 us (level)
  Pallas kernels: 109 us -> 105 us
  local copies, waits for them, and re-layouts: 0 us -> 3.94 us
    pallas_call x2 -> x1, Pallas kernels: 109 us -> 105 us  [step(): pl.pallas_call(main_kernel, in_specs=[smem, anywhere, anywhere, anywhere,...]
    unnamed x0 -> x1, local copies, waits for them, and re-layouts: none -> 3.94 us
where the time goes in v6:
time: 109 us
  Pallas kernels  105 us (96%)
  local copies, waits for them, and re-layouts  3.94 us (4%)
    pallas_call x1, Pallas kernels, step(): pl.pallas_call(main_kernel, in_specs=[smem, anywhere, anywhere, anywhere,...  105 us
    unnamed x1, local copies, waits for them, and re-layouts  3.94 us

profile of v6, /device:TPU:1, one launch (start us, length us, event | category | flops | bytes accessed | tf_op | source)
XLA Modules:
  0.0 108.7 jit_solution(3761276253993192561)
XLA Ops:
  0.0 104.7 %step.1 = f32[12,20,4,641]{3,2,1,0:T(4,128)} custom-call(s32[2,4]{1,0:T(2,128)} %bitcast.5, f32[12,20,4,641]{3,2,1,0:T(4,128)} %bitcast.4, bf16[20,641,384]{2,1,0:T(8,128)(2,1)} %leg_any.1, bf16[1280,1280]{1,0:T(8,128)(2,1)} %constant.4.clone.tall_any, bf16[1280,1280]{1,0:T(8,128)(2,1)} %constant.5.clone.wide_any, f32[384]{0:T(512)} %sin_ref.1, ...), custom_call_target="tpu_custom_call" | custom-call | tf_op jit(solution)/shard_map/step/pallas_call | solution.py:680
  104.8 3.9 %copy.10 = f32[4,12,20,641]{3,0,2,1:T(4,128)} copy(f32[4,12,20,641]{3,0,2,1:T(4,128)} %bitcast.3) | data formatting | bytes 4922880

commit v7 on v6

--- a/solution.py
+++ b/solution.py
@@ -23,7 +23,8 @@
 GROUPS = LOCAL // GROUP
 FULL = 128 * FIELDS
 LANES = FULL + 64 * FIELDS
-PART = ((0, FULL), (FULL, LANES))
+PART = ((0, FULL), (FULL, LANES), (0, LANES))
+BOTH = 2
 MEMBERS = 8
 CHIPS = 4
 KILLED = 4
@@ -310,11 +311,8 @@
 def spread(axis, count, body):
     me = lax.axis_index(axis)
 
-    def one(d, _):
-        body(lax.rem(me + d, count))
-        return 0
-
-    lax.fori_loop(1, count, one, 0)
+    for d in range(1, count):
+        body((me + d) & (count - 1))
 
 
 def main_kernel(
@@ -354,6 +352,8 @@
     rs_recv,
     ag_send,
     ag_recv,
+    over_send,
+    over_recv,
     out_send,
     out_recv,
     back_send,
@@ -420,20 +420,27 @@
 
     def gather(q, g, peer, source):
         return pltpu.make_async_remote_copy(
-            src_ref=shared_ref.at[q, g, source & 1, source >> 1],
-            dst_ref=shared_ref.at[q, g, source & 1, source >> 1],
+            src_ref=shared_ref.at[q, g, core, source],
+            dst_ref=shared_ref.at[q, g, core, source],
             send_sem=ag_send.at[q, g, peer],
             recv_sem=ag_recv.at[q, g, source],
-            device_id={"member": peer},
+            device_id={"member": 2 * peer + core},
             device_id_type=MESH,
         )
 
+    def hand_over(q, g, half):
+        return pltpu.make_async_remote_copy(
+            src_ref=shared_ref.at[q, g, half],
+            dst_ref=shared_ref.at[q, g, half],
+            send_sem=over_send.at[q, g],
+            recv_sem=over_recv.at[q, g],
+            device_id={"member": partner},
+            device_id_type=MESH,
+        )
+
     def other_chips(body):
-        def one(d, _):
-            body(lax.rem(chip + d, CHIPS))
-            return 0
-
-        lax.fori_loop(1, CHIPS, one, 0)
+        for d in range(1, CHIPS):
+            body((chip + d) & (CHIPS - 1))
 
     def regroup(g):
         rows = jnp.concatenate(
@@ -467,12 +474,16 @@
         other_chips(lambda peer: scatter(q, g, peer, peer).wait_recv())
         total = pair_ref[q, g, chip].astype(F32)
         for d in range(1, CHIPS):
-            total = total + landed_ref[q, g, lax.rem(chip + d, CHIPS)].astype(F32)
+            total = total + landed_ref[q, g, (chip + d) & (CHIPS - 1)].astype(F32)
         shared_ref[q, g, core, chip] = total.astype(BF16)
-        spread("member", MEMBERS, lambda peer: gather(q, g, peer, member).start())
+        other_chips(lambda peer: gather(q, g, peer, chip).start())
+
+    def forward(q, g):
+        other_chips(lambda peer: gather(q, g, peer, peer).wait_recv())
+        hand_over(q, g, core).start()
 
     def arrived(q, g):
-        spread("member", MEMBERS, lambda peer: gather(q, g, peer, peer).wait_recv())
+        hand_over(q, g, 1 - core).wait_recv()
 
     def received(q, g):
         return jnp.concatenate(
@@ -489,8 +500,8 @@
         return pltpu.make_async_remote_copy(
             src_ref=send_ref.at[g, peer, :, lanes],
             dst_ref=fourier_ref.at[pl.ds(g * TILE + source * 16, 16), lanes],
-            send_sem=out_send.at[part, g, peer],
-            recv_sem=out_recv.at[part, g, source],
+            send_sem=out_send.at[part % BOTH, g, peer],
+            recv_sem=out_recv.at[part % BOTH, g, source],
             device_id={"space": peer},
             device_id_type=MESH,
         )
@@ -515,12 +526,17 @@
         rows = pl.ds(g * TILE + place * 16, 16)
         return pltpu.make_async_copy(give_ref.at[rows], back_ref.at[g, place], own_sem.at[1, g])
 
-    def each_group(body):
+    def each_group(body, first=0, last=GROUPS):
         def one(g, _):
             body(g)
             return 0
 
-        lax.fori_loop(0, GROUPS, one, 0)
+        lax.fori_loop(first, last, one, 0)
+
+    def each_message(part, body):
+        if part == 0:
+            each_group(lambda g: body(BOTH, g), 0, EARLY)
+        each_group(lambda g: body(part, g), EARLY, GROUPS)
 
     def send_out(part, g):
         spread("space", SPACE, lambda peer: outward(part, g, peer, place).start())
@@ -534,28 +550,20 @@
     regroup(1)
     offer(0, 1)
     combine(0, 0)
+    keep, put_rows = keep_and_put(clones_ref, member)
+    combine(0, 1)
+    settle(0, 0)
     x_copy(2).wait()
     regroup(2)
     offer(0, 2)
-    combine(0, 1)
-    keep, put_rows = keep_and_put(clones_ref, member)
-    settle(0, 0)
+    settle(0, 1)
+    forward(0, 0)
+    x_copy(3).wait()
+    regroup(3)
+    offer(0, 3)
+    combine(0, 2)
 
     def legendre_step(g, _):
-        @pl.when(g + 3 < GROUPS)
-        def _():
-            x_copy(g + 3).wait()
-            regroup(g + 3)
-            offer(0, g + 3)
-
-        @pl.when(g + 2 < GROUPS)
-        def _():
-            combine(0, g + 2)
-
-        @pl.when(g + 1 < GROUPS)
-        def _():
-            settle(0, g + 1)
-
         arrived(0, g)
         now = jnp.dot(keep, half_ref[0, g], preferred_element_type=F32)
         now_ref[...] = now + jnp.dot(put_rows, received(0, g), preferred_element_type=F32)
@@ -567,12 +575,33 @@
         legendre_group(
             place * LOCAL + g * GROUP, now_ref, leg_ref.at[pl.ds(g * GROUP, GROUP)], put
         )
-        send_out(0, g)
-        own_out(g).start()
-
         @pl.when(g < EARLY)
         def _():
-            send_out(1, g)
+            send_out(BOTH, g)
+
+        @pl.when(g >= EARLY)
+        def _():
+            send_out(0, g)
+
+        own_out(g).start()
+
+        @pl.when(g + 2 < GROUPS)
+        def _():
+            settle(0, g + 2)
+
+        @pl.when(g + 3 < GROUPS)
+        def _():
+            combine(0, g + 3)
+
+        @pl.when(g + 1 < GROUPS)
+        def _():
+            forward(0, g + 1)
+
+        @pl.when(g + 4 < GROUPS)
+        def _():
+            x_copy(g + 4).wait()
+            regroup(g + 4)
+            offer(0, g + 4)
 
         return 0
 
@@ -590,10 +619,11 @@
     each_group(lambda g: own_out(g).wait())
 
     for part in range(2):
-        each_group(
-            lambda g: spread(
-                "space", SPACE, lambda peer: outward(part, g, peer, peer).wait_recv()
-            )
+        each_message(
+            part,
+            lambda kind, g: spread(
+                "space", SPACE, lambda peer: outward(kind, g, peer, peer).wait_recv()
+            ),
         )
         grid_forward(part, sines[part], fourier_ref, wide_ref, forcing_ref)
 
@@ -605,6 +635,8 @@
         each_group(backward)
         if part == 0:
             each_group(lambda g: settle(1, g))
+        else:
+            each_group(lambda g: forward(1, g))
     each_group(lambda g: own_back(g).start())
 
     placing = place_rows(clones_ref, member)
@@ -629,7 +661,6 @@
         return pltpu.make_async_copy(xg_ref.at[g], new_any.at[:, some], state_sem.at[g])
 
     def project(g):
-        complete(g)
         own_back(g).wait()
         for part in range(2):
             spread(
@@ -645,18 +676,19 @@
         )
         new_copy(g).start()
 
+    each_group(complete)
     each_group(project)
     for q in range(2):
         each_group(lambda g: across(q, g).wait_send())
         each_group(lambda g: other_chips(lambda peer: scatter(q, g, peer, chip).wait_send()))
-        each_group(
-            lambda g: spread("member", MEMBERS, lambda peer: gather(q, g, peer, member).wait_send())
-        )
+        each_group(lambda g: other_chips(lambda peer: gather(q, g, peer, chip).wait_send()))
+        each_group(lambda g: hand_over(q, g, core).wait_send())
     for part in range(2):
-        each_group(
-            lambda g: spread(
-                "space", SPACE, lambda peer: outward(part, g, peer, place).wait_send()
-            )
+        each_message(
+            part,
+            lambda kind, g: spread(
+                "space", SPACE, lambda peer: outward(kind, g, peer, place).wait_send()
+            ),
         )
         each_group(
             lambda g: spread(
@@ -708,8 +740,10 @@
             dma((2, GROUPS)),
             dma((2, GROUPS, CHIPS)),
             dma((2, GROUPS, CHIPS)),
-            dma((2, GROUPS, MEMBERS)),
-            dma((2, GROUPS, MEMBERS)),
+            dma((2, GROUPS, CHIPS)),
+            dma((2, GROUPS, CHIPS)),
+            dma((2, GROUPS)),
+            dma((2, GROUPS)),
             dma((2, GROUPS, SPACE)),
             dma((2, GROUPS, SPACE)),
             dma((2, GROUPS, SPACE)),

time: 109 us -> 107 us (0.982)
  Pallas kernels: 105 us -> 103 us
    pallas_call x1, Pallas kernels: 105 us -> 103 us  [step(): pl.pallas_call(main_kernel, in_specs=[smem, anywhere, anywhere, anywhere,...]
where the time goes in v7:
time: 107 us
  Pallas kernels  103 us (96%)
  local copies, waits for them, and re-layouts  3.94 us (4%)
    pallas_call x1, Pallas kernels, step(): pl.pallas_call(main_kernel, in_specs=[smem, anywhere, anywhere, anywhere,...  103 us
    unnamed x1, local copies, waits for them, and re-layouts  3.94 us

profile of v7, /device:TPU:1, one launch (start us, length us, event | category | flops | bytes accessed | tf_op | source)
XLA Modules:
  0.0 107.3 jit_solution(9535728890833704919)
XLA Ops:
  0.0 103.4 %step.1 = f32[12,20,4,641]{3,2,1,0:T(4,128)} custom-call(s32[2,4]{1,0:T(2,128)} %bitcast.5, f32[12,20,4,641]{3,2,1,0:T(4,128)} %bitcast.4, bf16[20,641,384]{2,1,0:T(8,128)(2,1)} %leg_any.1, bf16[1280,1280]{1,0:T(8,128)(2,1)} %constant.4.clone.tall_any, bf16[1280,1280]{1,0:T(8,128)(2,1)} %constant.5.clone.wide_any, f32[384]{0:T(512)} %sin_ref.1, ...), custom_call_target="tpu_custom_call" | custom-call | tf_op jit(solution)/shard_map/step/pallas_call | solution.py:712
  103.4 3.9 %copy.10 = f32[4,12,20,641]{3,0,2,1:T(4,128)} copy(f32[4,12,20,641]{3,0,2,1:T(4,128)} %bitcast.3) | data formatting | bytes 4922880

commit v8 on v7

--- a/solution.py
+++ b/solution.py
@@ -541,27 +541,22 @@
     def send_out(part, g):
         spread("space", SPACE, lambda peer: outward(part, g, peer, place).start())
 
-    x_copy(0).wait()
-    regroup(0)
+    keep, put_rows = keep_and_put(clones_ref, member)
+    for g in range(2):
+        x_copy(g).wait()
+        regroup(g)
     pl.semaphore_wait(barrier, SPACE + MEMBERS - 2)
     offer(0, 0)
-
-    x_copy(1).wait()
-    regroup(1)
     offer(0, 1)
     combine(0, 0)
-    keep, put_rows = keep_and_put(clones_ref, member)
     combine(0, 1)
     settle(0, 0)
     x_copy(2).wait()
     regroup(2)
     offer(0, 2)
     settle(0, 1)
+    combine(0, 2)
     forward(0, 0)
-    x_copy(3).wait()
-    regroup(3)
-    offer(0, 3)
-    combine(0, 2)
 
     def legendre_step(g, _):
         arrived(0, g)
@@ -589,19 +584,16 @@
         def _():
             settle(0, g + 2)
 
-        @pl.when(g + 3 < GROUPS)
-        def _():
-            combine(0, g + 3)
-
         @pl.when(g + 1 < GROUPS)
         def _():
             forward(0, g + 1)
 
-        @pl.when(g + 4 < GROUPS)
+        @pl.when(g + 3 < GROUPS)
         def _():
-            x_copy(g + 4).wait()
-            regroup(g + 4)
-            offer(0, g + 4)
+            x_copy(g + 3).wait()
+            regroup(g + 3)
+            offer(0, g + 3)
+            combine(0, g + 3)
 
         return 0
 

time: 107 us -> 106 us (level)
  Pallas kernels: 103 us -> 101 us
    pallas_call x1, Pallas kernels: 103 us -> 101 us  [step(): pl.pallas_call(main_kernel, in_specs=[smem, anywhere, anywhere, anywhere,...]
where the time goes in v8:
time: 106 us; the launch traced here: 105 us
  Pallas kernels  101 us (95%)
  local copies, waits for them, and re-layouts  3.94 us (4%)
    pallas_call x1, Pallas kernels, step(): pl.pallas_call(main_kernel, in_specs=[smem, anywhere, anywhere, anywhere,...  101 us
    unnamed x1, local copies, waits for them, and re-layouts  3.94 us

profile of v8, /device:TPU:1, one launch (start us, length us, event | category | flops | bytes accessed | tf_op | source)
XLA Modules:
  0.0 105.4 jit_solution(17708071876927402781)
XLA Ops:
  0.0 101.4 %step.1 = f32[12,20,4,641]{3,2,1,0:T(4,128)} custom-call(s32[2,4]{1,0:T(2,128)} %bitcast.5, f32[12,20,4,641]{3,2,1,0:T(4,128)} %bitcast.4, bf16[20,641,384]{2,1,0:T(8,128)(2,1)} %leg_any.1, bf16[1280,1280]{1,0:T(8,128)(2,1)} %constant.4.clone.tall_any, bf16[1280,1280]{1,0:T(8,128)(2,1)} %constant.5.clone.wide_any, f32[384]{0:T(512)} %sin_ref.1, ...), custom_call_target="tpu_custom_call" | custom-call | tf_op jit(solution)/shard_map/step/pallas_call | solution.py:704
  101.4 3.9 %copy.10 = f32[4,12,20,641]{3,0,2,1:T(4,128)} copy(f32[4,12,20,641]{3,0,2,1:T(4,128)} %bitcast.3) | data formatting | bytes 4922880

commit v9 on v8

--- a/solution.py
+++ b/solution.py
@@ -32,7 +32,7 @@
 GROUPED = (GROUPS, 2 * FIELDS, GROUP, TRAJ, WIDTH)
 MIX = 2 * FIELDS * GROUP
 TILE = 16 * SPACE
-EARLY = 2
+EARLY = 1
 MESH = pl.DeviceIdType.MESH
 DT = 0.25
 WAVE_SCALE = 16.0

time: 106 us -> 104 us (0.981)
  Pallas kernels: 101 us -> 99.7 us
    pallas_call x1, Pallas kernels: 101 us -> 99.7 us  [step(): pl.pallas_call(main_kernel, in_specs=[smem, anywhere, anywhere, anywhere,...]
where the time goes in v9:
time: 104 us
  Pallas kernels  99.7 us (96%)
  local copies, waits for them, and re-layouts  3.94 us (4%)
    pallas_call x1, Pallas kernels, step(): pl.pallas_call(main_kernel, in_specs=[smem, anywhere, anywhere, anywhere,...  99.7 us
    unnamed x1, local copies, waits for them, and re-layouts  3.94 us

profile of v9, /device:TPU:1, one launch (start us, length us, event | category | flops | bytes accessed | tf_op | source)
XLA Modules:
  0.0 103.7 jit_solution(10911707170939081572)
XLA Ops:
  0.0 99.7 %step.1 = f32[12,20,4,641]{3,2,1,0:T(4,128)} custom-call(s32[2,4]{1,0:T(2,128)} %bitcast.5, f32[12,20,4,641]{3,2,1,0:T(4,128)} %bitcast.4, bf16[20,641,384]{2,1,0:T(8,128)(2,1)} %leg_any.1, bf16[1280,1280]{1,0:T(8,128)(2,1)} %constant.4.clone.tall_any, bf16[1280,1280]{1,0:T(8,128)(2,1)} %constant.5.clone.wide_any, f32[384]{0:T(512)} %sin_ref.1, ...), custom_call_target="tpu_custom_call" | custom-call | tf_op jit(solution)/shard_map/step/pallas_call | solution.py:704
  99.7 3.9 %copy.10 = f32[4,12,20,641]{3,0,2,1:T(4,128)} copy(f32[4,12,20,641]{3,0,2,1:T(4,128)} %bitcast.3) | data formatting | bytes 4922880

commit v10 on v9

--- a/solution.py
+++ b/solution.py
@@ -32,7 +32,7 @@
 GROUPED = (GROUPS, 2 * FIELDS, GROUP, TRAJ, WIDTH)
 MIX = 2 * FIELDS * GROUP
 TILE = 16 * SPACE
-EARLY = 1
+EARLY = 0
 MESH = pl.DeviceIdType.MESH
 DT = 0.25
 WAVE_SCALE = 16.0

time: 104 us -> 105 us (level)
  Pallas kernels: 99.7 us -> 101 us
    pallas_call x1, Pallas kernels: 99.7 us -> 101 us  [step(): pl.pallas_call(main_kernel, in_specs=[smem, anywhere, anywhere, anywhere,...]
where the time goes in v10:
time: 105 us
  Pallas kernels  101 us (96%)
  local copies, waits for them, and re-layouts  3.94 us (4%)
    pallas_call x1, Pallas kernels, step(): pl.pallas_call(main_kernel, in_specs=[smem, anywhere, anywhere, anywhere,...  101 us
    unnamed x1, local copies, waits for them, and re-layouts  3.94 us

profile of v10, /device:TPU:1, one launch (start us, length us, event | category | flops | bytes accessed | tf_op | source)
XLA Modules:
  0.0 105.3 jit_solution(4829205610108805686)
XLA Ops:
  0.0 101.4 %step.1 = f32[12,20,4,641]{3,2,1,0:T(4,128)} custom-call(s32[2,4]{1,0:T(2,128)} %bitcast.5, f32[12,20,4,641]{3,2,1,0:T(4,128)} %bitcast.4, bf16[20,641,384]{2,1,0:T(8,128)(2,1)} %leg_any.1, bf16[1280,1280]{1,0:T(8,128)(2,1)} %constant.4.clone.tall_any, bf16[1280,1280]{1,0:T(8,128)(2,1)} %constant.5.clone.wide_any, f32[384]{0:T(512)} %sin_ref.1, ...), custom_call_target="tpu_custom_call" | custom-call | tf_op jit(solution)/shard_map/step/pallas_call | solution.py:704
  101.4 3.9 %copy.10 = f32[4,12,20,641]{3,0,2,1:T(4,128)} copy(f32[4,12,20,641]{3,0,2,1:T(4,128)} %bitcast.3) | data formatting | bytes 4922880
